TPU v7x, 128 devices: a whole 4x4x4 slice. The times are simulated.
128 devices in a mesh: lev: 4 (over x), sub: 32 (over z, y, core).
Axes of the slice: x: 4, y: 4, z: 4, core: 2. Of those that a mesh axis runs over, the one named last changes fastest.
Arguments:
- length_x: float32 [32, 128], P('lev', 'sub'), may hold values from 2 to 200
- length_y: float32 [3072, 32], P(('lev', 'sub')), may hold values from 2 to 128
- length_z: float32 [3072, 128], P(('lev', 'sub')), may hold values from 1 to 32
- sigma: float32 [3072, 32, 128], P(('lev', 'sub')), may hold values from 0.3 to 3
- obs_profile: bfloat16 [32, 1048576], P(None, ('lev', 'sub')), may hold values from -1 to 1
- obs_scale: float32 [1048576], P(('lev', 'sub')), may hold values from 0.3 to 3
- innovation: bfloat16 [1048576], P(('lev', 'sub')), may hold values from -6 to 6
- obs_column: int32 [1048576], P(('lev', 'sub')), may hold values from 0 to 393215, as said below
- obs_count: int32 [128, 128], replicated, may hold values from 1 to 64, as said below
Outputs:
- control: float32 [32, 128, 3072], P('lev', 'sub')
- increment: float32 [3072, 32, 128], P(('lev', 'sub'))
- departures: float32 [1048576], P(('lev', 'sub'))
Inputs may be any that keep to these rules, and one draw needn't show every extreme that they name: `obs_column`: slot o names a column whose x lies among the 24 columns numbered from ((o // 64) % 128) * 24. `obs_count`: every sending device has a block with all 64 slots live, and one owner receives full blocks from every device.
All inputs are finite; a program needn't handle non-finite values.
Results may differ from a plain program's by a relative error of at most 0.0029.
Values may be sent and summed in bfloat16 or wider, within the bound.
A program may use at most 128 MiB of HBM per device.

v0:
```python
import jax
import jax.numpy as jnp
from jax import lax
from jax.sharding import PartitionSpec as P

ITERS = 2


def coefficients(length):
    decay = jnp.exp(-1.0 / length)
    square = decay * decay
    gain = jnp.power(1.0 - square, 0.75) / jnp.power(1.0 + square, 0.25)
    return (decay, gain)


def power_table(log_decay, extent):
    positions = jnp.arange(extent, dtype=jnp.int32)
    offsets = (positions[:, None] - positions[None, :]).astype(jnp.float32)
    lower_part = offsets >= 0.0
    powers = jnp.exp(log_decay[:, :, None] * jnp.maximum(offsets, 0.0)[None, :, :])
    return jnp.where(lower_part[None, :, :], powers, 0.0)


def block_sweep(values, log_decay, reverse):
    rows_all, block_count, block_len = values.shape
    within = power_table(log_decay, block_len)
    across = power_table(log_decay * block_len, block_count)
    positions = jnp.arange(block_len, dtype=jnp.float32)
    if reverse:
        local = jnp.einsum("rji,rkj->rki", within, values, precision=lax.Precision.HIGHEST)
        carried = jnp.einsum("rmk,rm->rk", across, local[:, :, 0], precision=lax.Precision.HIGHEST)
        following = jnp.concatenate([carried[:, 1:], jnp.zeros((rows_all, 1), jnp.float32)], axis=1)
        reach = jnp.exp(log_decay[:, :, None] * (block_len - positions)[None, None, :])
        return local + reach * following[:, :, None]
    local = jnp.einsum("rij,rkj->rki", within, values, precision=lax.Precision.HIGHEST)
    carried = jnp.einsum("rkm,rm->rk", across, local[:, :, -1], precision=lax.Precision.HIGHEST)
    previous = jnp.concatenate([jnp.zeros((rows_all, 1), jnp.float32), carried[:, :-1]], axis=1)
    reach = jnp.exp(log_decay[:, :, None] * (positions + 1.0)[None, None, :])
    return local + reach * previous[:, :, None]


def smooth_last(field, length):
    shape = field.shape
    extent = shape[-1]
    block_len = 128
    rows_all = length.size
    flat_length = length.reshape(rows_all, 1)
    log_decay = -1.0 / flat_length
    gain = coefficients(flat_length)[1]
    values = field.reshape(rows_all, extent // block_len, block_len) * gain[:, :, None]
    onward = block_sweep(values, log_decay, False)
    backward = block_sweep(onward * gain[:, :, None], log_decay, True)
    return backward.reshape(shape)


def smooth_levels(field, pair):
    decay, gain = pair
    level_count = field.shape[1]
    onward = []
    running = gain * field[:, 0, :]
    onward.append(running)
    for level in range(1, level_count):
        running = decay * running + gain * field[:, level, :]
        onward.append(running)
    result = [None] * level_count
    running = gain * onward[level_count - 1]
    result[level_count - 1] = running
    for level in range(level_count - 2, -1, -1):
        running = decay * running + gain * onward[level]
        result[level] = running
    return jnp.stack(result, axis=1)


def global_sums(values):
    return lax.psum(jnp.stack(values), ("lev", "sub"))


def body(
    length_x, length_y, length_z, sigma, obs_profile, obs_scale, innovation, obs_column, obs_count
):
    lev_count = lax.axis_size("lev")
    sub_count = lax.axis_size("sub")
    blocks = lev_count * sub_count
    cols_block, levels_all, rows_total = sigma.shape
    width_all = cols_block * blocks
    levels_dev = levels_all // lev_count
    rows_dev = rows_total // sub_count
    payload = cols_block * levels_dev * rows_dev
    pair_z = coefficients(length_z)

    def to_rows(field):
        pieces = field.reshape(cols_block, lev_count, levels_dev, sub_count, rows_dev).transpose(
            1, 3, 0, 2, 4
        )
        pieces = pieces.reshape(blocks, payload)
        moved = lax.all_to_all(pieces, ("lev", "sub"), split_axis=0, concat_axis=0, tiled=True)
        moved = moved.reshape(blocks, cols_block, levels_dev, rows_dev).transpose(2, 3, 0, 1)
        return moved.reshape(levels_dev, rows_dev, width_all)

    def adjoint_u(field):
        columns = smooth_last(smooth_levels(sigma * field, pair_z), length_y)
        return smooth_last(to_rows(columns), length_x)

    owner_index = lax.axis_index(("lev", "sub"))
    weights = (obs_scale[None, :] * obs_profile.astype(jnp.float32)).astype(jnp.bfloat16)
    got_weights, got_innov = (
        lax.all_to_all(weights, ("lev", "sub"), split_axis=1, concat_axis=1, tiled=True),
        lax.all_to_all(
            innovation.reshape(1, -1), ("lev", "sub"), split_axis=1, concat_axis=1, tiled=True
        ),
    )
    got_column = lax.all_to_all(obs_column, ("lev", "sub"), split_axis=0, concat_axis=0, tiled=True)
    slots_all = got_column.shape[0]
    capacity = slots_all // blocks
    local_col = got_column % width_all - owner_index * cols_block
    local_row = got_column // width_all
    counts = lax.dynamic_slice_in_dim(obs_count, owner_index, 1, 1)[:, 0]
    slot_range = jnp.arange(capacity, dtype=jnp.int32)
    live_mask = (slot_range[None, :] < counts[:, None]).astype(jnp.float32).reshape(slots_all)
    weight_float = got_weights.astype(jnp.float32)
    innov = live_mask * got_innov[0].astype(jnp.float32)
    col_onehot = (local_col[None, :] == jnp.arange(cols_block, dtype=jnp.int32)[:, None]).astype(
        jnp.float32
    )
    row_onehot = (local_row[:, None] == jnp.arange(rows_total, dtype=jnp.int32)[None, :]).astype(
        jnp.float32
    )

    def spread(values):
        placed = col_onehot[:, None, :] * (weight_float * values[None, :])[None, :, :]
        return jnp.einsum("czs,sr->czr", placed, row_onehot, precision=lax.Precision.HIGHEST)

    rhs = adjoint_u(spread(innov))
    control = jnp.zeros_like(rhs)
    increment = jnp.zeros_like(sigma)
    hinc = jnp.zeros((slots_all,), jnp.float32)
    residual = rhs
    direction = rhs
    norm_now = global_sums([jnp.sum(residual * residual)])[0]
    for step in range(ITERS):
        to_pieces = (
            smooth_last(direction, length_x)
            .reshape(levels_dev, rows_dev, blocks, cols_block)
            .transpose(2, 3, 0, 1)
        )
        to_pieces = to_pieces.reshape(blocks, payload)
        to_moved = lax.all_to_all(
            to_pieces, ("lev", "sub"), split_axis=0, concat_axis=0, tiled=True
        )
        to_moved = to_moved.reshape(
            lev_count, sub_count, cols_block, levels_dev, rows_dev
        ).transpose(2, 0, 3, 1, 4)
        forward_columns = to_moved.reshape(cols_block, levels_all, rows_total)
        image_u = sigma * smooth_levels(smooth_last(forward_columns, length_y), pair_z)
        picked = jnp.einsum("czr,sr->czs", image_u, row_onehot, precision=lax.Precision.HIGHEST)
        observe_values = jnp.sum(col_onehot[:, None, :] * picked, axis=0)
        image_obs = live_mask * jnp.sum(weight_float * observe_values, axis=0)
        image = direction + adjoint_u(spread(image_obs))
        curvature = global_sums([jnp.sum(direction * image)])[0]
        alpha = norm_now / curvature
        control = control + alpha * direction
        increment = increment + alpha * image_u
        hinc = hinc + alpha * image_obs
        residual = residual - alpha * image
        norm_next = global_sums([jnp.sum(residual * residual)])[0]
        direction = residual + norm_next / norm_now * direction
        norm_now = norm_next
    departures = hinc - innov
    return (control, increment, departures)


def solution(mesh):
    placed = (
        P("lev", "sub"),
        P(("lev", "sub"), None),
        P(("lev", "sub"), None),
        P(("lev", "sub"), None, None),
        P(None, ("lev", "sub")),
        P(("lev", "sub")),
        P(("lev", "sub")),
        P(("lev", "sub")),
        P(),
    )
    return jax.shard_map(
        body,
        mesh=mesh,
        in_specs=placed,
        out_specs=(P("lev", "sub", None), P(("lev", "sub"), None, None), P(("lev", "sub"))),
        check_vma=False,
    )
```

profile of v0, /device:TPU:1, one launch (start us, length us, event | category | flops | bytes accessed | tf_op | source)
XLA Modules:
  0.0 1325.4 jit_solution(13442265256624499551)
XLA Ops:
  47.5 12.2 all-to-all-done.1
  65.3 12.7 fusion.488
  78.0 16.7 %fusion.83 = f32[24,32,128]{2,1,0:T(8,128)} fusion(f32[24,32,128]{2,1,0:T(8,128)S(1)} %copy-done.3, s32[8192]{0:T(1024)S(1)} %get-tuple-element.211, f32[24,32,8192]{2,1,0:T(8,128)} %fusion.488), kind=kOutput, calls=%fused_computation.85 | convolution fusion | flops 9664823296 | bytes 25985024 | tf_op jit(solution)/shard_map/czs,sr->czr/dot_general | solution.py:131
  100.9 80.4 %fusion.9 = f32[768,1,128]{2,1,0:T(1,128)S(1)} fusion(f32[768,128,1]{1,2,0:T(1,128)S(1)} %bitcast.1869, f32[128,128]{1,0:T(8,128)S(1)} %convert_maximum_fusion, f32[768]{0:T(1024)S(1)} %div.114, pred[128,128]{1,0:T(8,128)(4,1)S(1)} %convert_compare_fusion), kind=kOutput, calls=%fused_computation.10 | convolution fusion | flops 176160768 | bytes 871424 | tf_op jit(solution)/shard_map/rij,rkj->rki/dot_general | solution.py:35
  181.6 44.5 %fusion.8 = f32[768,1,128]{2,1,0:T(1,128)S(1)} fusion(f32[768,128,1]{1,2,0:T(1,128)S(1)} %bitcast.1879, f32[128,128]{1,0:T(8,128)S(1)} %convert_maximum_fusion, f32[768]{0:T(1024)S(1)} %div.114, pred[128,128]{1,0:T(8,128)(4,1)S(1)} %convert_compare_fusion), kind=kOutput, calls=%fused_computation.9 | convolution fusion | flops 176160768 | bytes 871424 | tf_op jit(solution)/shard_map/rji,rkj->rki/dot_general | solution.py:30
  303.4 17.7 %all_to_all.73 = f32[128,1,768]{2,1,0:T(1,128)} all-to-all(f32[128,1,768]{2,1,0:T(1,128)} %copy.233), channel_id=1, replica_groups=mesh['lev'=4,'sub'=32] {'lev','sub'}, dimensions={0} | all-to-all | bytes 786432 | tf_op jit(solution)/shard_map/all_to_all | solution.py:147
  345.8 80.5 %fusion.7 = f32[768,1,128]{2,1,0:T(1,128)S(1)} fusion(f32[768,128,1]{1,2,0:T(1,128)S(1)} %bitcast.1870, f32[128,128]{1,0:T(8,128)S(1)} %convert_maximum_fusion, f32[768]{0:T(1024)S(1)} %div.114, pred[128,128]{1,0:T(8,128)(4,1)S(1)} %convert_compare_fusion), kind=kOutput, calls=%fused_computation.8 | convolution fusion | flops 176160768 | bytes 871424 | tf_op jit(solution)/shard_map/rij,rkj->rki/dot_general | solution.py:35
  426.6 44.7 %fusion.6 = f32[768,1,128]{2,1,0:T(1,128)S(1)} fusion(f32[768,128,1]{1,2,0:T(1,128)S(1)} %bitcast.1881, f32[128,128]{1,0:T(8,128)S(1)} %convert_maximum_fusion, f32[768]{0:T(1024)S(1)} %div.114, pred[128,128]{1,0:T(8,128)(4,1)S(1)} %convert_compare_fusion), kind=kOutput, calls=%fused_computation.7 | convolution fusion | flops 176160768 | bytes 871424 | tf_op jit(solution)/shard_map/rji,rkj->rki/dot_general | solution.py:30
  474.5 12.4 multiply_reduce_fusion.1
  493.3 12.7 fusion.486
  505.9 16.7 %fusion.12 = f32[24,32,128]{2,1,0:T(8,128)} fusion(s32[8192]{0:T(1024)S(1)} %get-tuple-element.211, f32[24,32,8192]{2,1,0:T(8,128)} %fusion.486), kind=kOutput, calls=%fused_computation.14 | convolution fusion | flops 9664724992 | bytes 25591808 | tf_op jit(solution)/shard_map/czs,sr->czr/dot_general | solution.py:131
  525.4 81.1 %fusion.5 = f32[768,1,128]{2,1,0:T(1,128)S(1)} fusion(f32[768,128,1]{1,2,0:T(1,128)S(1)} %bitcast.1871, f32[128,128]{1,0:T(8,128)S(1)} %copy-done.16, f32[768]{0:T(1024)S(1)} %div.114, pred[128,128]{1,0:T(8,128)(4,1)} %copy-done.20), kind=kOutput, calls=%fused_computation.6 | convolution fusion | flops 176160768 | bytes 871424 | tf_op jit(solution)/shard_map/rij,rkj->rki/dot_general | solution.py:35
  606.9 44.5 %fusion.4 = f32[768,1,128]{2,1,0:T(1,128)S(1)} fusion(f32[768,128,1]{1,2,0:T(1,128)S(1)} %bitcast.1884, f32[128,128]{1,0:T(8,128)S(1)} %copy-done.16, f32[768]{0:T(1024)S(1)} %div.114, pred[128,128]{1,0:T(8,128)(4,1)S(1)} %copy-done.21), kind=kOutput, calls=%fused_computation.5 | convolution fusion | flops 176160768 | bytes 871424 | tf_op jit(solution)/shard_map/rji,rkj->rki/dot_general | solution.py:30
  676.3 17.7 %all_to_all.74 = f32[128,1,768]{2,1,0:T(1,128)} all-to-all(f32[128,1,768]{2,1,0:T(1,128)} %copy.276), channel_id=1, replica_groups=mesh['lev'=4,'sub'=32] {'lev','sub'}, dimensions={0} | all-to-all | bytes 786432 | tf_op jit(solution)/shard_map/all_to_all | solution.py:96
  713.7 63.2 %all-reduce.10 = (f32[1]{0:T(128)}, f32[1]{0:T(128)}) all-reduce(f32[1]{0:T(128)} %bitcast.84, f32[1]{0:T(128)} %bitcast.249), channel_id=1, replica_groups=mesh['lev'=4,'sub'=32] {'lev','sub'}, use_global_device_ids=true, to_apply=%region_1.2 | all-reduce | flops 2 | bytes 16 | tf_op jit(solution)/shard_map/psum | solution.py:75
  780.0 62.9 %psum.30 = f32[1]{0:T(128)} all-reduce(f32[1]{0:T(128)} %bitcast.251), channel_id=1, replica_groups=mesh['lev'=4,'sub'=32] {'lev','sub'}, use_global_device_ids=true, to_apply=%region_7.8 | all-reduce | flops 1 | bytes 8 | tf_op jit(solution)/shard_map/psum | solution.py:75
  862.2 17.5 %all_to_all.75 = f32[128,1,768]{2,1,0:T(1,128)} all-to-all(f32[128,1,768]{2,1,0:T(1,128)} %copy.284), channel_id=1, replica_groups=mesh['lev'=4,'sub'=32] {'lev','sub'}, dimensions={0} | all-to-all | bytes 786432 | tf_op jit(solution)/shard_map/all_to_all | solution.py:147
  904.4 80.4 %fusion.3 = f32[768,1,128]{2,1,0:T(1,128)S(1)} fusion(f32[768,128,1]{1,2,0:T(1,128)S(1)} %bitcast.1872, f32[128,128]{1,0:T(8,128)S(1)} %copy-done.16, f32[768]{0:T(1024)S(1)} %div.114, pred[128,128]{1,0:T(8,128)(4,1)S(1)} %copy-done.21), kind=kOutput, calls=%fused_computation.4 | convolution fusion | flops 176160768 | bytes 871424 | tf_op jit(solution)/shard_map/rij,rkj->rki/dot_general | solution.py:35
  985.1 44.9 %fusion.2 = f32[768,1,128]{2,1,0:T(1,128)S(1)} fusion(f32[768,128,1]{1,2,0:T(1,128)S(1)} %bitcast.1887, f32[128,128]{1,0:T(8,128)S(1)} %copy-done.16, f32[768]{0:T(1024)S(1)} %div.114, pred[128,128]{1,0:T(8,128)(4,1)S(1)} %copy-done.21), kind=kOutput, calls=%fused_computation.3 | convolution fusion | flops 176160768 | bytes 871424 | tf_op jit(solution)/shard_map/rji,rkj->rki/dot_general | solution.py:30
  1033.2 12.4 multiply_reduce_fusion
  1062.3 15.9 %fusion.10 = f32[24,32,128]{2,1,0:T(8,128)S(1)} fusion(s32[8192]{0:T(1024)S(1)} %get-tuple-element.211, f32[24,32,8192]{2,1,0:T(8,128)} %fusion.484), kind=kOutput, calls=%fused_computation.11 | convolution fusion | flops 9664724992 | bytes 25591808 | tf_op jit(solution)/shard_map/czs,sr->czr/dot_general | solution.py:131
  1080.1 80.4 %fusion.1 = f32[768,1,128]{2,1,0:T(1,128)S(1)} fusion(f32[768,128,1]{1,2,0:T(1,128)S(1)} %bitcast.1873, f32[128,128]{1,0:T(8,128)S(1)} %copy-done.16, f32[768]{0:T(1024)S(1)} %div.114, pred[128,128]{1,0:T(8,128)(4,1)S(1)} %copy-done.22), kind=kOutput, calls=%fused_computation.2 | convolution fusion | flops 176160768 | bytes 871424 | tf_op jit(solution)/shard_map/rij,rkj->rki/dot_general | solution.py:35
  1160.8 44.5 %fusion = f32[768,1,128]{2,1,0:T(1,128)S(1)} fusion(f32[768,128,1]{1,2,0:T(1,128)S(1)} %bitcast.1875, f32[128,128]{1,0:T(8,128)S(1)} %copy-done.16, f32[768]{0:T(1024)S(1)} %div.114, pred[128,128]{1,0:T(8,128)(4,1)S(1)} %copy-done.22), kind=kOutput, calls=%fused_computation.1 | convolution fusion | flops 176160768 | bytes 871424 | tf_op jit(solution)/shard_map/rji,rkj->rki/dot_general | solution.py:30
  1256.4 63.1 %psum.31 = f32[1]{0:T(128)} all-reduce(f32[1]{0:T(128)} %bitcast.417), channel_id=1, replica_groups=mesh['lev'=4,'sub'=32] {'lev','sub'}, use_global_device_ids=true, to_apply=%region_11.12 | all-reduce | flops 1 | bytes 8 | tf_op jit(solution)/shard_map/psum | solution.py:75
  (411 shorter events, 338.9 us)
Async XLA Ops:
  2.1 20.9 %all-to-all-start.2 = ((bf16[1,128,64]{2,0,1:T(2,128)(2,1)}), bf16[1,128,64]{2,0,1:T(2,128)(2,1)S(1)}, u32[]{:S(2)}, u32[]{:S(2)}) async-start(bf16[1,128,64]{2,0,1:T(2,128)(2,1)} %all_to_all.64), calls=%async_computation.2 | async-start | bytes 131072 | tf_op jit(solution)/shard_map/all_to_all | solution.py:108
  13.6 413.0 %copy-start.15 = (f32[128,128]{1,0:T(8,128)}, f32[128,128]{1,0:T(8,128)S(1)}, u32[]{:S(2)}) copy-start(f32[128,128]{1,0:T(8,128)S(1)} %convert_maximum_fusion) | copy-start | bytes 196612
  13.7 412.9 %copy-start.20 = (pred[128,128]{1,0:T(8,128)(4,1)}, pred[128,128]{1,0:T(8,128)(4,1)S(1)}, u32[]{:S(2)}) copy-start(pred[128,128]{1,0:T(8,128)(4,1)S(1)} %convert_compare_fusion) | copy-start | bytes 49156
  15.7 62.3 %copy-start.30 = (f32[32]{0:T(128)}, f32[32]{0:T(128)S(1)}, u32[]{:S(2)}) copy-start(f32[32]{0:T(128)S(1)} %div.117) | copy-start | bytes 388
  17.4 408.9 %copy-start.17 = (f32[128]{0:T(128)}, f32[128]{0:T(128)S(1)}, u32[]{:S(2)}) copy-start(f32[128]{0:T(128)S(1)} %get-tuple-element.217) | copy-start | bytes 1540
  23.0 18.3 %all-to-all-start = ((s32[128,64,1]{1,2,0:T(1,128)}), s32[128,64,1]{1,2,0:T(1,128)S(1)}, u32[]{:S(2)}, u32[]{:S(2)}) async-start(s32[128,64,1]{1,2,0:T(1,128)} %bitcast), calls=%async_computation | async-start | bytes 131072 | tf_op jit(solution)/shard_map/all_to_all | solution.py:112
  41.4 18.3 %all-to-all-start.1 = ((bf16[128,2,1024]{2,1,0:T(2,128)(2,1)}), bf16[128,2,1024]{2,1,0:T(2,128)(2,1)S(1)}, u32[]{:S(2)}, u32[]{:S(2)}) async-start(bf16[128,2,1024]{2,1,0:T(2,128)(2,1)} %reshape.623), calls=%async_computation.1 | async-start | bytes 1048576 | tf_op jit(solution)/shard_map/all_to_all | solution.py:107
  229.0 52.2 %copy-start.34 = (f32[32]{0:T(128)S(1)}, f32[32]{0:T(128)}, u32[]{:S(2)}) copy-start(f32[32]{0:T(128)} %get-tuple-element.214) | copy-start | bytes 388
  250.6 17.5 %all-to-all-start.3 = ((f32[128,1,768]{2,1,0:T(1,128)}), f32[128,1,768]{2,1,0:T(1,128)}, u32[]{:S(2)}, u32[]{:S(2)}) async-start(f32[128,1,768]{2,1,0:T(1,128)} %copy.224), calls=%async_computation.3 | async-start | bytes 786432 | tf_op jit(solution)/shard_map/all_to_all | solution.py:96
  256.1 64.9 %copy-start.27 = (pred[24,24]{1,0:T(8,128)(4,1)}, pred[24,24]{1,0:T(8,128)(4,1)S(1)}, u32[]{:S(2)}) copy-start(pred[24,24]{1,0:T(8,128)(4,1)S(1)} %convert_compare_fusion.1) | copy-start | bytes 1732
  256.2 64.9 %copy-start.25 = (f32[24,24]{1,0:T(8,128)}, f32[24,24]{1,0:T(8,128)S(1)}, u32[]{:S(2)}) copy-start(f32[24,24]{1,0:T(8,128)S(1)} %convert_maximum_fusion.1) | copy-start | bytes 6916
  525.4 81.2 %copy-start.18 = (f32[128]{0:T(128)S(1)}, f32[128]{0:T(128)}, u32[]{:S(2)}) copy-start(f32[128]{0:T(128)} %copy-done.17) | copy-start | bytes 1540
  525.4 81.5 %copy-start.21 = (pred[128,128]{1,0:T(8,128)(4,1)S(1)}, pred[128,128]{1,0:T(8,128)(4,1)}, u32[]{:S(2)}) copy-start(pred[128,128]{1,0:T(8,128)(4,1)} %copy-done.20) | copy-start | bytes 49156
  651.4 50.8 %copy-start.32 = (f32[32]{0:T(128)S(1)}, f32[32]{0:T(128)}, u32[]{:S(2)}) copy-start(f32[32]{0:T(128)} %copy-done.30) | copy-start | bytes 388
  651.4 50.8 %copy-start.38 = (f32[32]{0:T(128)S(1)}, f32[32]{0:T(128)}, u32[]{:S(2)}) copy-start(f32[32]{0:T(128)} %get-tuple-element.215) | copy-start | bytes 388
  654.3 52.5 %copy-start.26 = (f32[24,24]{1,0:T(8,128)S(1)}, f32[24,24]{1,0:T(8,128)}, u32[]{:S(2)}) copy-start(f32[24,24]{1,0:T(8,128)} %copy-done.25) | copy-start | bytes 6916
  654.3 52.5 %copy-start.28 = (pred[24,24]{1,0:T(8,128)(4,1)S(1)}, pred[24,24]{1,0:T(8,128)(4,1)}, u32[]{:S(2)}) copy-start(pred[24,24]{1,0:T(8,128)(4,1)} %copy-done.27) | copy-start | bytes 1732
  654.3 52.5 %copy-start.35 = (f32[32]{0:T(128)S(1)}, f32[32]{0:T(128)}, u32[]{:S(2)}) copy-start(f32[32]{0:T(128)} %get-tuple-element.214) | copy-start | bytes 388
  654.3 53.6 %copy-start.24 = (f32[32,128]{1,0:T(8,128)S(1)}, f32[32,128]{1,0:T(8,128)}, u32[]{:S(2)}) copy-start(f32[32,128]{1,0:T(8,128)} %copy-done.23) | copy-start | bytes 49156
  1080.1 80.4 %copy-start.19 = (f32[128]{0:T(128)S(1)}, f32[128]{0:T(128)}, u32[]{:S(2)}) copy-start(f32[128]{0:T(128)} %copy-done.17) | copy-start | bytes 1540
  1215.1 105.6 %copy-start.12 = (f32[8192]{0:T(1024)S(1)}, f32[8192]{0:T(1024)}, u32[]{:S(2)}) copy-start(f32[8192]{0:T(1024)} %copy-done.11) | copy-start | bytes 98308
  1215.1 105.6 %copy-start.14 = (f32[8192]{0:T(1024)S(1)}, f32[8192]{0:T(1024)}, u32[]{:S(2)}) copy-start(f32[8192]{0:T(1024)} %copy-done.13) | copy-start | bytes 98308
  1215.1 110.1 %copy-start.1 = (s32[128,128]{1,0:T(8,128)S(1)}, s32[128,128]{1,0:T(8,128)}, u32[]{:S(2)}) copy-start(s32[128,128]{1,0:T(8,128)} %param.17) | copy-start | bytes 196612
  1223.1 16.9 %all-to-all-start.7 = ((f32[128,1,768]{2,1,0:T(1,128)}), f32[128,1,768]{2,1,0:T(1,128)S(1)}, u32[]{:S(2)}, u32[]{:S(2)}) async-start(f32[128,1,768]{2,1,0:T(1,128)} %copy.327), calls=%async_computation.7 | async-start | bytes 786432 | tf_op jit(solution)/shard_map/all_to_all | solution.py:96
  (21 other events, 533.0 us)
where the time goes:
time: 1330 us
  matrix products  744 us (56%)
  blocking collectives  242 us (18%)
  local copies, waits for them, and re-layouts  177 us (13%)
  other arithmetic  75.6 us (6%)
  waiting for transfers between devices  44.1 us (3%)
  starting transfers between devices  35.6 us (3%)
    dot_general x10, matrix products, block_sweep(): jnp.einsum('rij,rkj->rki', within, values, precision=lax.Precision.HIGHEST)  425 us
    dot_general x10, matrix products, block_sweep(): jnp.einsum('rji,rkj->rki', within, values, precision=lax.Precision.HIGHEST)  235 us
    psum x3, blocking collectives, global_sums(): return lax.psum(jnp.stack(values), ('lev', 'sub'))  189 us
    dot_general x3, matrix products, spread(): jnp.einsum('czs,sr->czr', placed, row_onehot, precision=lax.Precision.HIG...  49.3 us
    dot_general x3, other arithmetic, spread(): jnp.einsum('czs,sr->czr', placed, row_onehot, precision=lax.Precision.HIG...  36.8 us
    all_to_all x2, blocking collectives, body(): lax.all_to_all(to_pieces, ('lev', 'sub'), split_axis=0, concat_axis=0, ti...  35.1 us
    another operation x7, local copies, waits for them, and re-layouts, smooth_last(): field.reshape(rows_all, extent // block_len, block_len) * gain[:, :, None]  31.5 us
    another operation x3, local copies, waits for them, and re-layouts, to_rows(): field.reshape(cols_block, lev_count, levels_dev, sub_count, rows_dev)  29.4 us
  transfers between devices with their start and end apart: 5, of which 5 were waited for; matrix products, arithmetic and copies ran while one was open for 1% of the time, Pallas kernels for 0%

commit v1 on v0

v1 whole, which is shorter than its diff:
```python
import functools

import jax
import jax.numpy as jnp
from jax import lax
from jax.experimental import pallas as pl
from jax.experimental.pallas import tpu as pltpu
from jax.sharding import PartitionSpec as P

MESH = pl.DeviceIdType.MESH
F32 = jnp.float32
BF16 = jnp.bfloat16
NLEV = 4
NSUB = 32
NDEV = NLEV * NSUB
NXB = 24
LEV = 32
NY = 128
CAP = 64
CELLS = NXB * LEV
NOBS = NDEV * CAP
HALF = NXB // 2
WROWS = HALF * LEV
TILES = NOBS // 128


def gain_of(decay):
    square = decay * decay
    below = jnp.sqrt(1.0 - square)
    return below * jnp.sqrt(below) / jnp.sqrt(jnp.sqrt(1.0 + square))


def chunked_loop(count, unroll, body):
    def step(i, carry):
        for k in range(unroll):
            body(i * unroll + k)
        return carry

    lax.fori_loop(0, count // unroll, step, 0)


def split(value):
    high = value.astype(BF16)
    return high, (value - high.astype(F32)).astype(BF16)


def kernel(
    prof_ref, scale_ref, meta_ref, sigma_ref, ly_ref, lz_ref,
    control_ref, increment_ref, dep_ref,
    ws, wl, ml, wide, rowhot, innov_ref, lenx_ref, dec_ref, gain_ref, resp_ref,
    pw, gy_ref, v, ubuf, x0, y0, x1, y1, tacc, fth, ftl, zs,
    es, el, cs, cr, cl, sc_src, sc_land,
    obs_send, obs_recv, edge_send, edge_recv, back_send, back_recv, sc_send, sc_recv,
):
    lev_i = lax.axis_index("lev")
    sub_i = lax.axis_index("sub")
    me = lev_i * NSUB + sub_i

    def device(index):
        return (index // NSUB, lax.rem(index, NSUB))

    def other(k):
        return lax.rem(me + k, NDEV)

    barrier = pltpu.get_barrier_semaphore()

    def greet(k, carry):
        pl.semaphore_signal(barrier, inc=1, device_id=device(other(k)), device_id_type=MESH)
        return carry

    lax.fori_loop(1, NDEV, greet, 0)

    lane = lax.broadcasted_iota(jnp.int32, (1, 128), 1)
    low_half = lane < CAP

    def pack(i, carry):
        at = pl.ds(pl.multiple_of(i * 128, 128), 128)
        w = prof_ref[:, at].astype(F32) * scale_ref[:, at]
        top, bottom = w[:16], w[16:]
        ws[2 * i] = jnp.where(low_half, top, pltpu.roll(bottom, CAP, 1)).astype(BF16)
        ws[2 * i + 1] = jnp.where(low_half, pltpu.roll(top, CAP, 1), bottom).astype(BF16)
        return carry

    lax.fori_loop(0, TILES, pack, 0)
    pl.semaphore_wait(barrier, NDEV - 1)

    def send_obs(k, carry):
        to = other(k)
        pltpu.make_async_remote_copy(
            src_ref=meta_ref.at[to], dst_ref=ml.at[me], send_sem=obs_send.at[0],
            recv_sem=obs_recv.at[0], device_id=device(to), device_id_type=MESH,
        ).start()
        pltpu.make_async_remote_copy(
            src_ref=ws.at[to], dst_ref=wl.at[me], send_sem=obs_send.at[1],
            recv_sem=obs_recv.at[1], device_id=device(to), device_id_type=MESH,
        ).start()
        return carry

    lax.fori_loop(1, NDEV, send_obs, 0)
    ml[me] = meta_ref[me]
    wl[me] = ws[me]

    decay_y = jnp.exp(-1.0 / ly_ref[...])
    gy_ref[...] = jnp.broadcast_to(gain_of(decay_y), (CELLS, 128))
    power = decay_y
    for k in range(7):
        pw[k] = jnp.broadcast_to(power, (CELLS, 128))
        power = power * power
    decay_z = jnp.exp(-1.0 / lz_ref[...])
    gain_z = gain_of(decay_z)

    def wait_all(src, dst, send_sem, recv_sem):
        copy = pltpu.make_async_remote_copy(
            src_ref=src, dst_ref=dst, send_sem=send_sem, recv_sem=recv_sem,
            device_id=(lev_i, sub_i), device_id_type=MESH,
        )
        copy.wait_recv()
        copy.wait_send()

    rest = pl.ds(0, NDEV - 1)
    wait_all(meta_ref.at[rest], ml.at[rest], obs_send.at[0], obs_recv.at[0])

    lengths = ml[:, 1, :]
    k_id = lax.broadcasted_iota(jnp.int32, (128, 128), 0)
    y_id = lax.broadcasted_iota(jnp.int32, (128, 128), 1)
    mine = (lax.rem(k_id, NSUB) == y_id // 4).astype(F32)
    for row in range(8):
        pick = (k_id == row * 4 + lax.rem(y_id, 4)).astype(F32)
        spread_row = jnp.dot(
            lengths, pick, precision=lax.Precision.HIGHEST, preferred_element_type=F32
        )
        rows = jnp.sum((spread_row * mine).reshape(NLEV, NSUB, 128), axis=1)
        lenx_ref[pl.ds(row, NLEV, stride=8), :] = rows
    decay_x = jnp.exp(-1.0 / lenx_ref[...])
    gain_x = gain_of(decay_x)
    dec_ref[...] = decay_x
    gain_ref[...] = gain_x

    level = pl.ds(sub_i, 1)
    a = dec_ref[level, :]
    g = gain_ref[level, :]
    up = [a]
    for _ in range(NXB - 1):
        up.append(up[-1] * a)

    def sweep(values):
        total = jnp.zeros_like(a)
        out = []
        for value in values:
            total = a * total + g * value
            out.append(total)
        return out

    block_decay = up[-1]
    p1 = sweep(up[::-1])[::-1]
    q1 = sweep(p1)
    q2 = sweep(up[::-1])
    r1 = sweep(q1[::-1])
    r2 = sweep(q2[::-1])
    for index, value in enumerate((block_decay, p1[0], q1[-1], q2[-1], r1[-1], r2[-1])):
        resp_ref[pl.ds(index, 1), :] = value

    wait_all(ws.at[rest], wl.at[rest], obs_send.at[1], obs_recv.at[1])

    place = lax.broadcasted_iota(jnp.int32, (256, 128), 0)

    def widen(i, carry):
        at = pl.ds(pl.multiple_of(i * 128, 128), 128)
        even, odd = wl[2 * i].astype(F32), wl[2 * i + 1].astype(F32)
        low = jnp.where(low_half, even, pltpu.roll(odd, CAP, 1))
        high = jnp.where(low_half, pltpu.roll(even, CAP, 1), odd)
        w = jnp.concatenate([low, high], axis=0)
        m_even, m_odd = ml[2 * i, pl.ds(0, 1), :], ml[2 * i + 1, pl.ds(0, 1), :]
        innov_ref[:, at] = jnp.where(low_half, m_even, pltpu.roll(m_odd, CAP, 1))
        key = jnp.where(low_half, pltpu.roll(m_even, CAP, 1), m_odd).astype(jnp.int32)
        spot = key // 16
        column = key - 16 * spot
        for c in range(HALF):
            wide[pl.ds(c * LEV, LEV), at] = jnp.where(column == c, w, 0.0).astype(BF16)
        rowhot[:, at] = jnp.where(place == spot, 1.0, 0.0).astype(BF16)
        return carry

    lax.fori_loop(0, TILES, widen, 0)

    CHUNK = 1024

    def spread(source, exact):
        tacc[...] = jnp.zeros_like(tacc)

        def step(i, carry):
            at = pl.ds(pl.multiple_of(i * CHUNK, CHUNK), CHUNK)
            hot = rowhot[:, at]
            parts = split(source[:, at])
            if exact:
                parts = parts[:1]
            total = tacc[...]
            for part in parts:
                total += lax.dot_general(
                    wide[:, at], hot * part, (((1,), (1,)), ((), ())),
                    preferred_element_type=F32,
                )
            tacc[...] = total
            return carry

        lax.fori_loop(0, NOBS // CHUNK, step, 0)

    def observe(field, out):
        side = jnp.concatenate([field[pl.ds(0, WROWS), :], field[pl.ds(WROWS, WROWS), :]], axis=1)
        fth[...], ftl[...] = split(side.T)

        def step(i, carry):
            at = pl.ds(pl.multiple_of(i * CHUNK, CHUNK), CHUNK)
            w = wide[:, at]
            got = jnp.dot(fth[...], w, preferred_element_type=F32)
            got += jnp.dot(ftl[...], w, preferred_element_type=F32)
            out[:, at] = jnp.sum(got * rowhot[:, at].astype(F32), axis=0, keepdims=True)
            return carry

        lax.fori_loop(0, NOBS // CHUNK, step, 0)

    def filter_z(ref):
        def row(z):
            return pl.ds(z, NXB, stride=LEV)

        def onward(i, total):
            for k in range(8):
                z = i * 8 + k
                total = decay_z * total + gain_z * ref[row(z), :]
                ref[row(z), :] = total
            return total

        def backward(i, total):
            for k in range(8):
                z = LEV - 1 - (i * 8 + k)
                total = decay_z * total + gain_z * ref[row(z), :]
                ref[row(z), :] = total
            return total

        lax.fori_loop(0, LEV // 8, onward, jnp.zeros((NXB, 128), F32))
        lax.fori_loop(0, LEV // 8, backward, jnp.zeros((NXB, 128), F32))

    YROWS = 128

    def filter_y(ref):
        def step(i, carry):
            at = pl.ds(pl.multiple_of(i * YROWS, YROWS), YROWS)
            gain = gy_ref[at, :]
            value = gain * ref[at, :]
            for k in range(7):
                moved = jnp.where(lane >= (1 << k), pltpu.roll(value, 1 << k, 1), 0.0)
                value = value + pw[k, at, :] * moved
            value = gain * value
            for k in range(7):
                moved = jnp.where(
                    lane < 128 - (1 << k), pltpu.roll(value, 128 - (1 << k), 1), 0.0
                )
                value = value + pw[k, at, :] * moved
            ref[at, :] = value
            return carry

        lax.fori_loop(0, CELLS // YROWS, step, 0)

    def sweep_x(src, dst, start, reverse):
        decay, gain = dec_ref[...], gain_ref[...]

        def step(i, total):
            for k in range(6):
                c = i * 6 + k
                if reverse:
                    c = NXB - 1 - c
                at = pl.ds(pl.multiple_of(c * LEV, LEV), LEV)
                total = decay * total + gain * src[at, :]
                dst[at, :] = total
            return total

        return lax.fori_loop(0, NXB // 6, step, start)

    def scan(values, reverse):
        sub = lax.broadcasted_iota(jnp.int32, (NDEV, 1), 0)
        factor = resp_ref[pl.ds(0, 1), :]
        for k in range(7):
            d = 1 << k
            if reverse:
                moved = jnp.where(sub < NDEV - d, pltpu.roll(values, NDEV - d, 0), 0.0)
            else:
                moved = jnp.where(sub >= d, pltpu.roll(values, d, 0), 0.0)
            values = values + factor * moved
            factor = factor * factor
        if reverse:
            return jnp.where(sub < NDEV - 1, pltpu.roll(values, NDEV - 1, 0), 0.0)
        return jnp.where(sub >= 1, pltpu.roll(values, 1, 0), 0.0)

    def covariance(turn, x_out, y_out):
        v[pl.ds(0, WROWS), :] = tacc[:, pl.ds(0, 128)] * sigma_ref[pl.ds(0, WROWS), :]
        v[pl.ds(WROWS, WROWS), :] = tacc[:, pl.ds(128, 128)] * sigma_ref[pl.ds(WROWS, WROWS), :]
        filter_z(v)
        filter_y(v)
        zero = jnp.zeros((LEV, 128), F32)
        es[:, 0, :] = sweep_x(v, ubuf, zero, False)
        es[:, 1, :] = sweep_x(ubuf, ubuf, zero, True)
        es[:, 2, :] = sweep_x(ubuf, ubuf, zero, False)
        es[:, 3, :] = sweep_x(ubuf, ubuf, zero, True)

        def send_edges(k, carry):
            to = other(k)
            pltpu.make_async_remote_copy(
                src_ref=es.at[lax.rem(to, NSUB)], dst_ref=el.at[turn, me],
                send_sem=edge_send.at[turn], recv_sem=edge_recv.at[turn],
                device_id=device(to), device_id_type=MESH,
            ).start()
            return carry

        lax.fori_loop(1, NDEV, send_edges, 0)
        el[turn, me] = es[sub_i]
        wait_all(el.at[turn, rest], el.at[turn, rest], edge_send.at[turn], edge_recv.at[turn])

        e1, e2 = el[turn, :, 0, :], el[turn, :, 1, :]
        e3, e4 = el[turn, :, 2, :], el[turn, :, 3, :]
        _, k1, k2, k3, k4, k5 = [resp_ref[pl.ds(i, 1), :] for i in range(6)]
        c1 = scan(e1, False)
        c2 = scan(e2 + k1 * c1, True)
        c3 = scan(e3 + k2 * c1 + k3 * c2, False)
        c4 = scan(e4 + k4 * c1 + k5 * c2 + k1 * c3, True)
        group = pl.ds(pl.multiple_of(lev_i * NSUB, NSUB), NSUB)
        for index, value in enumerate((c1, c2, c3, c4)):
            cs[...] = value
            cr[:, index, :] = cs[group, :]

        def send_back(k, carry):
            to = lax.rem(sub_i + k, NSUB)
            pltpu.make_async_remote_copy(
                src_ref=cr.at[to], dst_ref=cl.at[turn, sub_i],
                send_sem=back_send.at[turn], recv_sem=back_recv.at[turn],
                device_id=(lev_i, to), device_id_type=MESH,
            ).start()
            return carry

        lax.fori_loop(1, NSUB, send_back, 0)
        cl[turn, sub_i] = cr[sub_i]
        back = pl.ds(0, NSUB - 1)
        wait_all(cl.at[turn, back], cl.at[turn, back], back_send.at[turn], back_recv.at[turn])
        sweep_x(v, v, cl[turn, :, 0, :], False)
        sweep_x(v, x_out, cl[turn, :, 1, :], True)
        sweep_x(x_out, v, cl[turn, :, 2, :], False)
        sweep_x(v, y_out, cl[turn, :, 3, :], True)
        filter_y(y_out)
        filter_z(y_out)
        y_out[...] = y_out[...] * sigma_ref[...]

    def share(turn, sums):
        row = jnp.zeros((1, 128), F32)
        for index, value in enumerate(sums):
            row = jnp.where(lane == index, value, row)
        sc_src[turn] = row

        def go(k, carry):
            pltpu.make_async_remote_copy(
                src_ref=sc_src.at[turn], dst_ref=sc_land.at[turn, me],
                send_sem=sc_send.at[turn], recv_sem=sc_recv.at[turn],
                device_id=device(other(k)), device_id_type=MESH,
            ).start()
            return carry

        lax.fori_loop(1, NDEV, go, 0)
        sc_land[turn, me] = row

    def collect(turn, count):
        wait_all(
            sc_land.at[turn, rest], sc_land.at[turn, rest], sc_send.at[turn], sc_recv.at[turn]
        )
        total = jnp.sum(sc_land[turn, :, 0, :], axis=0, keepdims=True)
        return [
            jnp.sum(jnp.where(lane == index, total, 0.0), axis=1, keepdims=True)
            for index in range(count)
        ]

    def dot(left, right):
        return jnp.sum(jnp.sum(left * right, axis=0, keepdims=True), axis=1, keepdims=True)

    zrow0, zrow1 = zs.at[pl.ds(0, 1)], zs.at[pl.ds(1, 1)]
    spread(innov_ref, True)
    covariance(0, x0, y0)
    observe(y0, zrow0)
    z0 = zrow0[...]
    share(0, [dot(x0[...], x0[...]), dot(z0, z0)])
    spread(zrow0, False)
    covariance(1, x1, y1)
    rr0, zz0 = collect(0, 2)
    alpha0 = rr0 / (rr0 + zz0)
    x1[...] = (1.0 - alpha0) * x0[...] - alpha0 * x1[...]
    y1[...] = (1.0 - alpha0) * y0[...] - alpha0 * y1[...]
    observe(y1, zrow1)
    z1 = zrow1[...]
    share(1, [dot(x1[...], x1[...]), dot(x1[...], x0[...]), dot(z1, z1), dot(z1, z0)])
    rr1, cross, zz1, zcross = collect(1, 4)
    beta = rr1 / rr0
    curvature = rr1 + zz1 + 2.0 * beta * (cross + zcross) + beta * beta * (rr0 + zz0)
    alpha1 = rr1 / curvature
    old = alpha0 + alpha1 * beta
    control_ref[...] = old * x0[...] + alpha1 * x1[...]
    increment_ref[...] = old * y0[...] + alpha1 * y1[...]
    dep_ref[...] = old * z0 + alpha1 * z1 - innov_ref[...]


def body(
    length_x, length_y, length_z, sigma, obs_profile, obs_scale, innovation, obs_column, obs_count
):
    me = lax.axis_index(("lev", "sub"))
    width = NXB * NDEV
    counts = lax.dynamic_slice_in_dim(obs_count, me, 1, 0)[0]
    live = jnp.arange(CAP, dtype=jnp.int32)[None, :] < counts[:, None]
    scale = jnp.where(live, obs_scale.reshape(NDEV, CAP), 0.0).reshape(1, NOBS)
    innov = jnp.where(live, innovation.reshape(NDEV, CAP).astype(F32), 0.0)
    column = obs_column.reshape(NDEV, CAP)
    local = column % width - NXB * jnp.arange(NDEV, dtype=jnp.int32)[:, None]
    half = local // HALF
    spot = half * NY + column // width
    key = (spot * 16 + (local - HALF * half)).astype(F32)
    lengths = jnp.pad(length_x.reshape(1, 32), ((0, 0), (0, 96)))
    meta = jnp.stack(
        [jnp.concatenate([innov, key], axis=1), jnp.broadcast_to(lengths, (NDEV, 128))], axis=1
    )
    vmem = pl.BlockSpec(memory_space=pltpu.VMEM)
    field = pltpu.VMEM((CELLS, 128), F32)
    control, increment, departures = pl.pallas_call(
        kernel,
        out_shape=(
            jax.ShapeDtypeStruct((CELLS, 128), F32),
            jax.ShapeDtypeStruct((CELLS, 128), F32),
            jax.ShapeDtypeStruct((1, NOBS), F32),
        ),
        in_specs=[vmem] * 6,
        out_specs=(vmem,) * 3,
        scratch_shapes=[
            pltpu.VMEM((NDEV, 16, 128), BF16),
            pltpu.VMEM((NDEV, 16, 128), BF16),
            pltpu.VMEM((NDEV, 2, 128), F32),
            pltpu.VMEM((WROWS, NOBS), BF16),
            pltpu.VMEM((256, NOBS), BF16),
            pltpu.VMEM((1, NOBS), F32),
            pltpu.VMEM((LEV, 128), F32),
            pltpu.VMEM((LEV, 128), F32),
            pltpu.VMEM((LEV, 128), F32),
            pltpu.VMEM((8, 128), F32),
            pltpu.VMEM((7, CELLS, 128), F32),
            field,
            field,
            field,
            field,
            field,
            field,
            field,
            pltpu.VMEM((WROWS, 256), F32),
            pltpu.VMEM((256, WROWS), BF16),
            pltpu.VMEM((256, WROWS), BF16),
            pltpu.VMEM((2, NOBS), F32),
            pltpu.VMEM((LEV, 4, 128), F32),
            pltpu.VMEM((2, NDEV, 4, 128), F32),
            pltpu.VMEM((NDEV, 128), F32),
            pltpu.VMEM((NSUB, 4, 128), F32),
            pltpu.VMEM((2, LEV, 4, 128), F32),
            pltpu.VMEM((2, 1, 128), F32),
            pltpu.VMEM((2, NDEV, 1, 128), F32),
            pltpu.SemaphoreType.DMA((2,)),
            pltpu.SemaphoreType.DMA((2,)),
            pltpu.SemaphoreType.DMA((2,)),
            pltpu.SemaphoreType.DMA((2,)),
            pltpu.SemaphoreType.DMA((2,)),
            pltpu.SemaphoreType.DMA((2,)),
            pltpu.SemaphoreType.DMA((2,)),
            pltpu.SemaphoreType.DMA((2,)),
        ],
        compiler_params=pltpu.CompilerParams(
            collective_id=0, has_side_effects=True, vmem_limit_bytes=56 << 20
        ),
    )(
        obs_profile, scale, meta, sigma.reshape(CELLS, 128), length_y.reshape(CELLS, 1), length_z
    )
    pieces = control.reshape(NXB, NLEV, LEV // NLEV, NSUB, NY // NSUB).transpose(1, 3, 0, 2, 4)
    moved = lax.all_to_all(
        pieces.reshape(NDEV, -1), ("lev", "sub"), split_axis=0, concat_axis=0, tiled=True
    )
    rows = moved.reshape(NDEV, NXB, LEV // NLEV, NY // NSUB).transpose(2, 3, 0, 1)
    return (
        rows.reshape(LEV // NLEV, NY // NSUB, width),
        increment.reshape(NXB, LEV, NY),
        departures.reshape(NOBS),
    )


def solution(mesh):
    blocks = P(("lev", "sub"))
    placed = (
        P("lev", "sub"), blocks, blocks, blocks, P(None, ("lev", "sub")),
        blocks, blocks, blocks, P(),
    )
    return jax.shard_map(
        body,
        mesh=mesh,
        in_specs=placed,
        out_specs=(P("lev", "sub", None), blocks, blocks),
        check_vma=False,
    )
```

time: 1330 us -> 175 us (0.13)
  matrix products: 744 us -> 0 us
  blocking collectives: 242 us -> 0 us
  local copies, waits for them, and re-layouts: 177 us -> 26.4 us
  Pallas kernels: 0 us -> 123 us
  other arithmetic: 75.6 us -> 4.12 us
  waiting for transfers between devices: 44.1 us -> 12.1 us
  starting transfers between devices: 35.6 us -> 7.06 us
    dot_general x35 -> x0, matrix products: 744 us -> none  [the longest x10 425 us: block_sweep(): jnp.einsum('rij,rkj->rki', within, values, precision=lax.Precision.HIGHEST)]
    psum x3 -> x0, blocking collectives: 189 us -> none  [global_sums(): return lax.psum(jnp.stack(values), ('lev', 'sub'))]
    pallas_call x0 -> x1, Pallas kernels: none -> 123 us  [body(): pl.pallas_call(kernel, out_shape=(jax.ShapeDtypeStruct((CELLS, 128), F32)...]
    another operation x15 -> x1, local copies, waits for them, and re-layouts: 68 us -> 0.04 us  [body(): jnp.stack([jnp.concatenate([innov, key], axis=1), jnp.broadcast_to(length...]
    all_to_all x3 -> x0, blocking collectives: 52.8 us -> none  [the longest x2 35.1 us: body(): lax.all_to_all(to_pieces, ('lev', 'sub'), split_axis=0, concat_axis=0, ti...]
    transpose x10 -> x1, local copies, waits for them, and re-layouts: 49.2 us -> 6.14 us  [body(): control.reshape(NXB, NLEV, LEV // NLEV, NSUB, NY // NSUB)]
    dot_general x3 -> x0, other arithmetic: 36.8 us -> none  [spread(): jnp.einsum('czs,sr->czr', placed, row_onehot, precision=lax.Precision.HIG...]
    all_to_all x5 -> x1, waiting for transfers between devices: 44.1 us -> 12.1 us  [body(): lax.all_to_all(pieces.reshape(NDEV, -1), ('lev', 'sub'), split_axis=0, co...]
  transfers between devices with their start and end apart: 5 -> 1, of which waited for: 5 -> 1; matrix products, arithmetic and copies ran while one was open for 1% -> 0% of each run, Pallas kernels for 0% -> 0%
where the time goes in v1:
time: 175 us; the launch traced here: 174 us
  Pallas kernels  123 us (70%)
  local copies, waits for them, and re-layouts  26.4 us (15%)
  waiting for transfers between devices  12.1 us (7%)
  starting transfers between devices  7.06 us (4%)
  other arithmetic  4.12 us (2%)
    pallas_call x1, Pallas kernels, body(): pl.pallas_call(kernel, out_shape=(jax.ShapeDtypeStruct((CELLS, 128), F32)...  123 us
    all_to_all x1, waiting for transfers between devices, body(): lax.all_to_all(pieces.reshape(NDEV, -1), ('lev', 'sub'), split_axis=0, co...  12.1 us
    reshape x1, local copies, waits for them, and re-layouts, body(): control.reshape(NXB, NLEV, LEV // NLEV, NSUB, NY // NSUB)  9.2 us
    all_to_all x1, starting transfers between devices, body(): lax.all_to_all(pieces.reshape(NDEV, -1), ('lev', 'sub'), split_axis=0, co...  7.06 us
    transpose x1, local copies, waits for them, and re-layouts, body(): control.reshape(NXB, NLEV, LEV // NLEV, NSUB, NY // NSUB)  6.14 us
    unnamed x11, local copies, waits for them, and re-layouts  4.78 us
  transfers between devices with their start and end apart: 1, of which 1 were waited for; matrix products, arithmetic and copies ran while one was open for 0% of the time, Pallas kernels for 0%

profile of v1, /device:TPU:1, one launch (start us, length us, event | category | flops | bytes accessed | tf_op | source)
XLA Modules:
  0.0 173.9 jit_solution(15237314392988169655)
XLA Ops:
  0.7 0.8 sign_compare_fusion.1
  1.5 0.8 broadcast_remainder_fusion
  2.3 0.8 copy.19
  3.1 0.1 ne.39
  3.2 0.1 iota_compare_fusion
  3.3 0.1 lt.34
  3.4 0.8 reshape.77
  4.4 1.9 %reshape.78.ly_ref = f32[768,1]{1,0:T(8,128)} reshape(f32[24,32]{1,0:T(8,128)} %param.10) | data formatting | bytes 6144 | tf_op jit(solution)/shard_map/reshape | solution.py:477
  6.3 1.4 broadcast_select_fusion.1
  7.7 0.1 fusion.4
  7.9 0.8 pad_maximum_fusion.meta_ref
  8.7 123.4 %shard_map.112 = (f32[768,128]{1,0:T(8,128)}, f32[768,128]{1,0:T(8,128)}, f32[1,8192]{1,0:T(1,128)}) custom-call(bf16[32,8192]{1,0:T(8,128)(2,1)} %prof_ref.1, f32[1,8192]{1,0:T(1,128)} %bitcast.24, f32[128,2,128]{2,1,0:T(2,128)} %pad_maximum_fusion.meta_ref, f32[768,128]{1,0:T(8,128)} %bitcast.22, f32[768,1]{1,0:T(8,128)} %reshape.78.ly_ref, f32[24,128]{1,0:T(8,128)} %lz_ref.1), custom_call_target="tpu_custom_call" | custom-call | tf_op jit(solution)/shard_map/pallas_call | solution.py:425
  132.1 1.2 copy.21
  133.3 9.2 %reshape.72 = f32[24,4,8,32,4]{2,1,0,4,3:T(4,128)} reshape(f32[768,128]{0,1:T(8,128)S(1)} %copy.21) | data formatting | bytes 786432 | tf_op jit(solution)/shard_map/reshape | solution.py:479
  142.5 6.1 %copy.22 = f32[4,32,24,8,4]{1,0,4,3,2:T(4,128)S(1)} copy(f32[4,32,24,8,4]{3,0,2,4,1:T(4,128)} %bitcast.19) | data formatting | bytes 786432 | tf_op jit(solution)/shard_map/transpose | solution.py:479
  148.6 0.7 all_to_all.6
  149.3 1.0 copy.23
  150.3 7.1 %all-to-all-start = ((f32[128,1,768]{2,1,0:T(1,128)}), f32[128,1,768]{2,1,0:T(1,128)S(1)}, u32[]{:S(2)}, u32[]{:S(2)}) async-start(f32[128,1,768]{2,1,0:T(1,128)} %copy.23), calls=%async_computation | async-start | bytes 786432 | tf_op jit(solution)/shard_map/all_to_all | solution.py:480
  157.4 12.1 %all-to-all-done = f32[128,1,768]{2,1,0:T(1,128)S(1)} async-done(((f32[128,1,768]{2,1,0:T(1,128)}), f32[128,1,768]{2,1,0:T(1,128)S(1)}, u32[]{:S(2)}, u32[]{:S(2)}) %all-to-all-start) | async-done | bytes 393248 | tf_op jit(solution)/shard_map/all_to_all | solution.py:480
  169.5 0.4 copy.24
  169.9 0.6 copy.27
  170.5 2.0 %reshape.79 = f32[8,4,3072]{2,1,0:T(4,128)} reshape(f32[8,4,128,24]{3,2,1,0:T(8,128)S(1)} %copy.27) | data formatting | bytes 786432
  172.6 0.7 copy.31
  173.3 0.6 copy.32
  (15 shorter events, 0.5 us)
Async XLA Ops:
  0.6 2.6 %copy-start = (s32[128,128]{1,0:T(8,128)S(1)}, s32[128,128]{1,0:T(8,128)}, u32[]{:S(2)}) copy-start(s32[128,128]{1,0:T(8,128)} %param.17) | copy-start | bytes 196612
  150.3 19.2 %all-to-all-start = ((f32[128,1,768]{2,1,0:T(1,128)}), f32[128,1,768]{2,1,0:T(1,128)S(1)}, u32[]{:S(2)}, u32[]{:S(2)}) async-start(f32[128,1,768]{2,1,0:T(1,128)} %copy.23), calls=%async_computation | async-start | bytes 786432 | tf_op jit(solution)/shard_map/all_to_all | solution.py:480
  169.9 2.7 %copy-start.1 = (f32[768,128]{1,0:T(8,128)S(1)}, f32[768,128]{1,0:T(8,128)}, u32[]{:S(2)}) copy-start(f32[768,128]{1,0:T(8,128)} %get-tuple-element.7) | copy-start | bytes 1179652
  170.5 2.8 %copy-start.2 = (f32[1,8192]{1,0:T(1,128)S(1)}, f32[1,8192]{1,0:T(1,128)}, u32[]{:S(2)}) copy-start(f32[1,8192]{1,0:T(1,128)} %get-tuple-element.8) | copy-start | bytes 98308

commit v2 on v1

v2 whole, which is shorter than its diff:
```python
import functools

import jax
import jax.numpy as jnp
from jax import lax
from jax.experimental import pallas as pl
from jax.experimental.pallas import tpu as pltpu
from jax.sharding import PartitionSpec as P

MESH = pl.DeviceIdType.MESH
F32 = jnp.float32
BF16 = jnp.bfloat16
NLEV = 4
NSUB = 32
NDEV = NLEV * NSUB
NXB = 24
LEV = 32
NY = 128
CAP = 64
CELLS = NXB * LEV
NOBS = NDEV * CAP
HALF = NXB // 2
WROWS = HALF * LEV
TILES = NOBS // 128
GROUPS = 4


def gain_of(decay):
    square = decay * decay
    below = jnp.sqrt(1.0 - square)
    return below * jnp.sqrt(below) / jnp.sqrt(jnp.sqrt(1.0 + square))


def chunked_loop(count, unroll, body):
    def step(i, carry):
        for k in range(unroll):
            body(i * unroll + k)
        return carry

    lax.fori_loop(0, count // unroll, step, 0)


def split(value):
    high = value.astype(BF16)
    return high, (value - high.astype(F32)).astype(BF16)


def kernel(
    lx_ref, ly_ref, lz_ref, sigma_ref, prof_ref, scale_ref, raw_ref, col_ref, count_ref,
    control_ref, increment_ref, dep_ref,
    live_ref, ms, ws, wl, ml, wide, rowhot, innov_ref, lenx_ref, dec_ref, gain_ref, resp_ref,
    pw, gy_ref, v, ubuf, vbuf, x0, y0, x1, y1, tacc, fth, ftl, zs,
    es, el, cs, cr, cl, sc_src, sc_land, tx1, ta, tx2, tb,
    meta_send, meta_recv, obs_send, obs_recv, edge_send, edge_recv, back_send, back_recv,
    sc_send, sc_recv, one_send, one_recv, two_send, two_recv,
):
    lev_i = lax.axis_index("lev")
    sub_i = lax.axis_index("sub")
    me = lev_i * NSUB + sub_i

    def device(index):
        return (index // NSUB, lax.rem(index, NSUB))

    def other(k):
        return lax.rem(me + k, NDEV)

    barrier = pltpu.get_barrier_semaphore()

    def greet(k, carry):
        pl.semaphore_signal(barrier, inc=1, device_id=device(other(k)), device_id_type=MESH)
        return carry

    lax.fori_loop(1, NDEV, greet, 0)

    lane = lax.broadcasted_iota(jnp.int32, (1, 128), 1)
    low_half = lane < CAP

    def wait_all(src, dst, send_sem, recv_sem):
        copy = pltpu.make_async_remote_copy(
            src_ref=src, dst_ref=dst, send_sem=send_sem, recv_sem=recv_sem,
            device_id=(lev_i, sub_i), device_id_type=MESH,
        )
        copy.wait_recv()
        copy.wait_send()

    rest = pl.ds(0, NDEV - 1)

    counts = jnp.broadcast_to(count_ref[pl.ds(me, 1), :], (TILES, 128))
    owner = lax.broadcasted_iota(jnp.int32, (TILES, 128), 1)
    tile = lax.broadcasted_iota(jnp.int32, (TILES, 128), 0)
    even_count = jnp.sum(jnp.where(owner == 2 * tile, counts, 0), axis=1, keepdims=True)
    odd_count = jnp.sum(jnp.where(owner == 2 * tile + 1, counts, 0), axis=1, keepdims=True)
    live = jnp.where(owner < CAP, owner, owner - CAP) < jnp.where(owner < CAP, even_count, odd_count)
    live_ref[...] = jnp.where(live, scale_ref[...], 0.0)
    innov_sent = jnp.where(live, raw_ref[...].astype(F32), 0.0)
    column = col_ref[...].astype(F32)
    row = jnp.floor((column + 0.5) * (1.0 / (NXB * NDEV)))
    first = (2 * tile + jnp.where(owner < CAP, 0, 1)) * NXB
    local = column - row * (NXB * NDEV) - first.astype(F32)
    half = jnp.where(local >= HALF, 1.0, 0.0)
    key_sent = (half * NY + row) * 16.0 + (local - HALF * half)
    even = jnp.where(low_half, innov_sent, pltpu.roll(key_sent, CAP, 1))
    odd = jnp.where(low_half, pltpu.roll(innov_sent, CAP, 1), key_sent)
    ms[:, 0, :] = jnp.stack([even, odd], axis=1).reshape(NDEV, 128)
    pick4 = (
        lax.broadcasted_iota(jnp.int32, (4, 128), 0)
        == lax.rem(lax.broadcasted_iota(jnp.int32, (4, 128), 1), 4)
    ).astype(F32)
    own = jnp.dot(
        lx_ref[...], pick4, precision=lax.Precision.HIGHEST, preferred_element_type=F32
    )
    own_at = lax.broadcasted_iota(jnp.int32, (8, 128), 1) // 4
    own = jnp.where(own_at == lax.broadcasted_iota(jnp.int32, (8, 128), 0), own, 0.0)
    ms[:, 1, :] = jnp.broadcast_to(jnp.sum(own, axis=0, keepdims=True), (NDEV, 128))

    def pack(i, carry):
        at = pl.ds(pl.multiple_of(i * 128, 128), 128)
        w = prof_ref[:, at].astype(F32) * live_ref[pl.ds(i, 1), :]
        top, bottom = w[:16], w[16:]
        ws[2 * i] = jnp.where(low_half, top, pltpu.roll(bottom, CAP, 1)).astype(BF16)
        ws[2 * i + 1] = jnp.where(low_half, pltpu.roll(top, CAP, 1), bottom).astype(BF16)
        return carry

    lax.fori_loop(0, TILES, pack, 0)
    pl.semaphore_wait(barrier, NDEV - 1)

    pair, core = me // 2, lax.rem(me, 2)
    PAIRS = TILES // GROUPS

    def send_block(kp, to_core):
        to_pair = lax.rem(pair + kp, TILES)
        to = 2 * to_pair + to_core
        group = kp // PAIRS
        pltpu.make_async_remote_copy(
            src_ref=ms.at[to], dst_ref=ml.at[me],
            send_sem=meta_send.at[group], recv_sem=meta_recv.at[group],
            device_id=device(to), device_id_type=MESH,
        ).start()
        pltpu.make_async_remote_copy(
            src_ref=ws.at[to], dst_ref=wl.at[me],
            send_sem=obs_send.at[group], recv_sem=obs_recv.at[group],
            device_id=device(to), device_id_type=MESH,
        ).start()

    send_block(0, 1 - core)

    def send_pair(kp, carry):
        send_block(kp, core)
        send_block(kp, 1 - core)
        return carry

    lax.fori_loop(1, TILES, send_pair, 0)
    ml[me] = ms[me]
    wl[me] = ws[me]

    decay_y = jnp.exp(-1.0 / ly_ref[...])
    gain_y = gain_of(decay_y).T
    decay_y = decay_y.T
    for c in range(NXB):
        rows = pl.ds(c * LEV, LEV)
        gy_ref[rows, :] = jnp.broadcast_to(gain_y[:, c:c + 1], (LEV, 128))
        power = jnp.broadcast_to(decay_y[:, c:c + 1], (LEV, 128))
        for k in range(7):
            pw[k, rows, :] = power
            power = power * power
    decay_z = jnp.exp(-1.0 / lz_ref[...])
    gain_z = gain_of(decay_z)

    place = lax.broadcasted_iota(jnp.int32, (256, 128), 0).astype(F32).astype(BF16)

    def widen(kp, carry):
        i = lax.rem(pair - kp + TILES, TILES)
        at = pl.ds(pl.multiple_of(i * 128, 128), 128)
        even, odd = wl[2 * i].astype(F32), wl[2 * i + 1].astype(F32)
        low = jnp.where(low_half, even, pltpu.roll(odd, CAP, 1))
        high = jnp.where(low_half, pltpu.roll(even, CAP, 1), odd)
        w = jnp.concatenate([low, high], axis=0).astype(BF16)
        m_even, m_odd = ml[2 * i, pl.ds(0, 1), :], ml[2 * i + 1, pl.ds(0, 1), :]
        innov_ref[:, at] = jnp.where(low_half, m_even, pltpu.roll(m_odd, CAP, 1))
        key = jnp.where(low_half, pltpu.roll(m_even, CAP, 1), m_odd)
        spot = jnp.floor(key * (1.0 / 16.0))
        column = jnp.broadcast_to(key - 16.0 * spot, (LEV, 128)).astype(BF16)
        for c in range(HALF):
            wide[pl.ds(c * LEV, LEV), at] = jnp.where(column == c, w, jnp.zeros_like(w))
        spot = jnp.broadcast_to(spot, (256, 128)).astype(BF16)
        rowhot[:, at] = jnp.where(place == spot, jnp.ones_like(place), jnp.zeros_like(place))
        return carry

    for group in range(GROUPS):
        blocks = pl.ds(0, 2 * PAIRS - (group == 0))
        wait_all(ms.at[blocks], ml.at[blocks], meta_send.at[group], meta_recv.at[group])
        wait_all(ws.at[blocks], wl.at[blocks], obs_send.at[group], obs_recv.at[group])
        lax.fori_loop(group * PAIRS, (group + 1) * PAIRS, widen, 0)

    lengths = ml[:, 1, :]
    k_id = lax.broadcasted_iota(jnp.int32, (128, 128), 0)
    y_id = lax.broadcasted_iota(jnp.int32, (128, 128), 1)
    mine = (lax.rem(k_id, NSUB) == y_id // 4).astype(F32)
    for row in range(8):
        pick = (k_id == row * 4 + lax.rem(y_id, 4)).astype(F32)
        spread_row = jnp.dot(
            lengths, pick, precision=lax.Precision.HIGHEST, preferred_element_type=F32
        )
        rows = jnp.sum((spread_row * mine).reshape(NLEV, NSUB, 128), axis=1)
        lenx_ref[pl.ds(row, NLEV, stride=8), :] = rows
    decay_x = jnp.exp(-1.0 / lenx_ref[...])
    gain_x = gain_of(decay_x)
    dec_ref[...] = decay_x
    gain_ref[...] = gain_x

    level = pl.ds(sub_i, 1)
    a = dec_ref[level, :]
    g = gain_ref[level, :]
    up = [a]
    for _ in range(NXB - 1):
        up.append(up[-1] * a)

    def sweep(values):
        total = jnp.zeros_like(a)
        out = []
        for value in values:
            total = a * total + g * value
            out.append(total)
        return out

    block_decay = up[-1]
    p1 = sweep(up[::-1])[::-1]
    q1 = sweep(p1)
    q2 = sweep(up[::-1])
    r1 = sweep(q1[::-1])
    r2 = sweep(q2[::-1])
    for index, value in enumerate((block_decay, p1[0], q1[-1], q2[-1], r1[-1], r2[-1])):
        resp_ref[pl.ds(index, 1), :] = value

    CHUNK = 2048

    def spread(source, exact):
        tacc[...] = jnp.zeros_like(tacc)

        def step(i, carry):
            at = pl.ds(pl.multiple_of(i * CHUNK, CHUNK), CHUNK)
            hot = rowhot[:, at]
            parts = split(source[:, at])
            if exact:
                parts = parts[:1]
            total = tacc[...]
            for part in parts:
                total += lax.dot_general(
                    wide[:, at], hot * part, (((1,), (1,)), ((), ())),
                    preferred_element_type=F32,
                )
            tacc[...] = total
            return carry

        lax.fori_loop(0, NOBS // CHUNK, step, 0)

    def observe(field, out):
        side = jnp.concatenate([field[pl.ds(0, WROWS), :], field[pl.ds(WROWS, WROWS), :]], axis=1)
        fth[...], ftl[...] = split(side.T)

        def step(i, carry):
            at = pl.ds(pl.multiple_of(i * CHUNK, CHUNK), CHUNK)
            w = wide[:, at]
            got = jnp.dot(fth[...], w, preferred_element_type=F32)
            got += jnp.dot(ftl[...], w, preferred_element_type=F32)
            out[:, at] = jnp.sum(got * rowhot[:, at].astype(F32), axis=0, keepdims=True)
            return carry

        lax.fori_loop(0, NOBS // CHUNK, step, 0)

    def filter_z(src, mid, dst):
        def row(z):
            return pl.ds(z, NXB, stride=LEV)

        total = jnp.zeros((NXB, 128), F32)
        for z in range(LEV):
            total = decay_z * total + gain_z * src[row(z), :]
            mid[row(z), :] = total
        total = jnp.zeros((NXB, 128), F32)
        for z in range(LEV - 1, -1, -1):
            total = decay_z * total + gain_z * mid[row(z), :]
            dst[row(z), :] = total

    def filter_y(src, dst):
        gain = gy_ref[...]
        value = gain * src[...]
        for k in range(7):
            moved = jnp.where(lane >= (1 << k), pltpu.roll(value, 1 << k, 1), 0.0)
            value = value + pw[k] * moved
        value = gain * value
        for k in range(7):
            moved = jnp.where(lane < 128 - (1 << k), pltpu.roll(value, 128 - (1 << k), 1), 0.0)
            value = value + pw[k] * moved
        dst[...] = value

    def sweep_x(src, dst, start, reverse):
        decay, gain = dec_ref[...], gain_ref[...]

        def step(i, total):
            for k in range(6):
                c = i * 6 + k
                if reverse:
                    c = NXB - 1 - c
                at = pl.ds(pl.multiple_of(c * LEV, LEV), LEV)
                total = decay * total + gain * src[at, :]
                dst[at, :] = total
            return total

        return lax.fori_loop(0, NXB // 6, step, start)

    def scan(values, reverse):
        sub = lax.broadcasted_iota(jnp.int32, (NDEV, 1), 0)
        factor = resp_ref[pl.ds(0, 1), :]
        for k in range(7):
            d = 1 << k
            if reverse:
                moved = jnp.where(sub < NDEV - d, pltpu.roll(values, NDEV - d, 0), 0.0)
            else:
                moved = jnp.where(sub >= d, pltpu.roll(values, d, 0), 0.0)
            values = values + factor * moved
            factor = factor * factor
        if reverse:
            return jnp.where(sub < NDEV - 1, pltpu.roll(values, NDEV - 1, 0), 0.0)
        return jnp.where(sub >= 1, pltpu.roll(values, 1, 0), 0.0)

    part = lax.rem(sub_i, 16)
    group_x = lev_i * 2 + sub_i // 16

    def exchange_one(turn, field):
        for z in range(LEV):
            tx1[turn, z // 2, pl.ds(z % 2 * NXB, NXB), :] = field[pl.ds(z, NXB, stride=LEV), :]

        def go(k, carry):
            to = lax.rem(part + k, 16)
            pltpu.make_async_remote_copy(
                src_ref=tx1.at[turn, to], dst_ref=ta.at[turn, part],
                send_sem=one_send.at[turn], recv_sem=one_recv.at[turn],
                device_id=(lev_i, sub_i - part + to), device_id_type=MESH,
            ).start()
            return carry

        lax.fori_loop(1, 16, go, 0)
        ta[turn, part] = tx1[turn, part]

    sub4 = lax.broadcasted_iota(jnp.int32, (1, 8, 1), 1) < 4
    to_lev = part // 4
    own_rows = lev_i == to_lev
    slot_two = pl.ds(pl.multiple_of(group_x * 384, 384), 384)

    def exchange_two(turn):
        fifteen = pl.ds(0, 15)
        wait_all(ta.at[turn, fifteen], ta.at[turn, fifteen], one_send.at[turn], one_recv.at[turn])
        lower = ta[turn, :, pl.ds(0, NXB), :].reshape(16 * NXB, 128).T.reshape(16, 8, 384)
        upper = ta[turn, :, pl.ds(NXB, NXB), :].reshape(16 * NXB, 128).T.reshape(16, 8, 384)
        even = jnp.where(sub4, lower, pltpu.roll(upper, 4, 1))
        odd = jnp.where(sub4, pltpu.roll(lower, 4, 1), upper)
        tx2[turn] = jnp.stack([even, odd], axis=1).reshape(NSUB, 8, 384)

        def send_rows(to):
            pltpu.make_async_remote_copy(
                src_ref=tx2.at[turn, to],
                dst_ref=tb.at[turn, lax.rem(part, 4), :, slot_two],
                send_sem=two_send.at[turn], recv_sem=two_recv.at[turn],
                device_id=(to_lev, to), device_id_type=MESH,
            ).start()

        def go(k, carry):
            send_rows(lax.rem(sub_i + k, NSUB))
            return carry

        lax.fori_loop(1, NSUB, go, 0)

        @pl.when(jnp.logical_not(own_rows))
        def _():
            send_rows(sub_i)

        @pl.when(own_rows)
        def _():
            tb[turn, lax.rem(part, 4), :, slot_two] = tx2[turn, sub_i]

    def finish_two(turn):
        @pl.when(own_rows)
        def _():
            most = tx2.at[turn, pl.ds(0, NSUB - 1)]
            wait_all(most, most, two_send.at[turn], two_recv.at[turn])

        @pl.when(jnp.logical_not(own_rows))
        def _():
            wait_all(tx2.at[turn], tx2.at[turn], two_send.at[turn], two_recv.at[turn])

    def covariance(turn, x_out, y_out):
        v[pl.ds(0, WROWS), :] = tacc[:, pl.ds(0, 128)] * sigma_ref[pl.ds(0, WROWS), :]
        v[pl.ds(WROWS, WROWS), :] = tacc[:, pl.ds(128, 128)] * sigma_ref[pl.ds(WROWS, WROWS), :]
        filter_z(v, ubuf, vbuf)
        filter_y(vbuf, v)
        zero = jnp.zeros((LEV, 128), F32)
        es[turn, :, 0, :] = sweep_x(v, ubuf, zero, False)
        es[turn, :, 1, :] = sweep_x(ubuf, vbuf, zero, True)
        es[turn, :, 2, :] = sweep_x(vbuf, ubuf, zero, False)
        es[turn, :, 3, :] = sweep_x(ubuf, vbuf, zero, True)

        def send_edges(k, carry):
            to = other(k)
            pltpu.make_async_remote_copy(
                src_ref=es.at[turn, lax.rem(to, NSUB)], dst_ref=el.at[turn, me],
                send_sem=edge_send.at[turn], recv_sem=edge_recv.at[turn],
                device_id=device(to), device_id_type=MESH,
            ).start()
            return carry

        lax.fori_loop(1, NDEV, send_edges, 0)
        el[turn, me] = es[turn, sub_i]
        if turn == 1:
            exchange_two(0)
        wait_all(el.at[turn, rest], el.at[turn, rest], edge_send.at[turn], edge_recv.at[turn])

        e1, e2 = el[turn, :, 0, :], el[turn, :, 1, :]
        e3, e4 = el[turn, :, 2, :], el[turn, :, 3, :]
        _, k1, k2, k3, k4, k5 = [resp_ref[pl.ds(i, 1), :] for i in range(6)]
        c1 = scan(e1, False)
        c2 = scan(e2 + k1 * c1, True)
        c3 = scan(e3 + k2 * c1 + k3 * c2, False)
        c4 = scan(e4 + k4 * c1 + k5 * c2 + k1 * c3, True)
        group = pl.ds(pl.multiple_of(lev_i * NSUB, NSUB), NSUB)
        for index, value in enumerate((c1, c2, c3, c4)):
            cs[...] = value
            cr[turn, :, index, :] = cs[group, :]

        def send_back(k, carry):
            to = lax.rem(sub_i + k, NSUB)
            pltpu.make_async_remote_copy(
                src_ref=cr.at[turn, to], dst_ref=cl.at[turn, sub_i],
                send_sem=back_send.at[turn], recv_sem=back_recv.at[turn],
                device_id=(lev_i, to), device_id_type=MESH,
            ).start()
            return carry

        lax.fori_loop(1, NSUB, send_back, 0)
        cl[turn, sub_i] = cr[turn, sub_i]
        back = pl.ds(0, NSUB - 1)
        wait_all(cl.at[turn, back], cl.at[turn, back], back_send.at[turn], back_recv.at[turn])
        sweep_x(v, ubuf, cl[turn, :, 0, :], False)
        sweep_x(ubuf, x_out, cl[turn, :, 1, :], True)
        exchange_one(turn, x_out)
        sweep_x(x_out, vbuf, cl[turn, :, 2, :], False)
        sweep_x(vbuf, ubuf, cl[turn, :, 3, :], True)
        filter_y(ubuf, vbuf)
        filter_z(vbuf, ubuf, v)
        y_out[...] = v[...] * sigma_ref[...]

    def share(turn, sums):
        row = jnp.zeros((1, 128), F32)
        for index, value in enumerate(sums):
            row = jnp.where(lane == index, value, row)
        sc_src[turn] = row

        def go(k, carry):
            pltpu.make_async_remote_copy(
                src_ref=sc_src.at[turn], dst_ref=sc_land.at[turn, me],
                send_sem=sc_send.at[turn], recv_sem=sc_recv.at[turn],
                device_id=device(other(k)), device_id_type=MESH,
            ).start()
            return carry

        lax.fori_loop(1, NDEV, go, 0)
        sc_land[turn, me] = row

    def collect(turn, count):
        wait_all(
            sc_land.at[turn, rest], sc_land.at[turn, rest], sc_send.at[turn], sc_recv.at[turn]
        )
        total = jnp.sum(sc_land[turn, :, 0, :], axis=0, keepdims=True)
        return [
            jnp.sum(jnp.where(lane == index, total, 0.0), axis=1, keepdims=True)
            for index in range(count)
        ]

    def dot(left, right):
        return jnp.sum(jnp.sum(left * right, axis=0, keepdims=True), axis=1, keepdims=True)

    zrow0, zrow1 = zs.at[pl.ds(0, 1)], zs.at[pl.ds(1, 1)]
    spread(innov_ref, True)
    covariance(0, x0, y0)
    observe(y0, zrow0)
    z0 = zrow0[...]
    share(0, [dot(x0[...], x0[...]), dot(z0, z0)])
    spread(zrow0, False)
    covariance(1, x1, y1)
    rr0, zz0 = collect(0, 2)
    alpha0 = rr0 / (rr0 + zz0)
    x1[...] = (1.0 - alpha0) * x0[...] - alpha0 * x1[...]
    y1[...] = (1.0 - alpha0) * y0[...] - alpha0 * y1[...]
    observe(y1, zrow1)
    z1 = zrow1[...]
    share(1, [dot(x1[...], x1[...]), dot(x1[...], x0[...]), dot(z1, z1), dot(z1, z0)])
    exchange_two(1)
    rr1, cross, zz1, zcross = collect(1, 4)
    beta = rr1 / rr0
    curvature = rr1 + zz1 + 2.0 * beta * (cross + zcross) + beta * beta * (rr0 + zz0)
    alpha1 = rr1 / curvature
    old = alpha0 + alpha1 * beta
    increment_ref[...] = old * y0[...] + alpha1 * y1[...]
    dep_ref[...] = old * z0 + alpha1 * z1 - innov_ref[...]
    finish_two(0)
    finish_two(1)
    control_ref[...] = (old + alpha1 * (1.0 - alpha0)) * tb[0] - (alpha1 * alpha0) * tb[1]


def body(
    length_x, length_y, length_z, sigma, obs_profile, obs_scale, innovation, obs_column, obs_count
):
    vmem = pl.BlockSpec(memory_space=pltpu.VMEM)
    field = pltpu.VMEM((CELLS, 128), F32)
    control, increment, departures = pl.pallas_call(
        kernel,
        out_shape=(
            jax.ShapeDtypeStruct((4, 8, NXB * NDEV), F32),
            jax.ShapeDtypeStruct((CELLS, 128), F32),
            jax.ShapeDtypeStruct((1, NOBS), F32),
        ),
        in_specs=[vmem] * 9,
        out_specs=(vmem,) * 3,
        scratch_shapes=[
            pltpu.VMEM((TILES, 128), F32),
            pltpu.VMEM((NDEV, 2, 128), F32),
            pltpu.VMEM((NDEV, 16, 128), BF16),
            pltpu.VMEM((NDEV, 16, 128), BF16),
            pltpu.VMEM((NDEV, 2, 128), F32),
            pltpu.VMEM((WROWS, NOBS), BF16),
            pltpu.VMEM((256, NOBS), BF16),
            pltpu.VMEM((1, NOBS), F32),
            pltpu.VMEM((LEV, 128), F32),
            pltpu.VMEM((LEV, 128), F32),
            pltpu.VMEM((LEV, 128), F32),
            pltpu.VMEM((8, 128), F32),
            pltpu.VMEM((7, CELLS, 128), F32),
            field,
            field,
            field,
            field,
            field,
            field,
            field,
            field,
            pltpu.VMEM((WROWS, 256), F32),
            pltpu.VMEM((256, WROWS), BF16),
            pltpu.VMEM((256, WROWS), BF16),
            pltpu.VMEM((2, NOBS), F32),
            pltpu.VMEM((2, LEV, 4, 128), F32),
            pltpu.VMEM((2, NDEV, 4, 128), F32),
            pltpu.VMEM((NDEV, 128), F32),
            pltpu.VMEM((2, NSUB, 4, 128), F32),
            pltpu.VMEM((2, LEV, 4, 128), F32),
            pltpu.VMEM((2, 1, 128), F32),
            pltpu.VMEM((2, NDEV, 1, 128), F32),
            pltpu.VMEM((2, 16, 2 * NXB, 128), F32),
            pltpu.VMEM((2, 16, 2 * NXB, 128), F32),
            pltpu.VMEM((2, NSUB, 8, 384), F32),
            pltpu.VMEM((2, 4, 8, NXB * NDEV), F32),
        ]
        + [pltpu.SemaphoreType.DMA((GROUPS,))] * 4
        + [pltpu.SemaphoreType.DMA((2,))] * 10,
        compiler_params=pltpu.CompilerParams(
            collective_id=0, has_side_effects=True, vmem_limit_bytes=56 << 20
        ),
    )(
        length_x, length_y, length_z, sigma.reshape(CELLS, 128), obs_profile,
        obs_scale.reshape(TILES, 128), innovation.reshape(TILES, 128),
        obs_column.reshape(TILES, 128), obs_count,
    )
    return (
        control.reshape(LEV // NLEV, NY // NSUB, NXB * NDEV),
        increment.reshape(NXB, LEV, NY),
        departures.reshape(NOBS),
    )


def solution(mesh):
    blocks = P(("lev", "sub"))
    placed = (
        P("lev", "sub"), blocks, blocks, blocks, P(None, ("lev", "sub")),
        blocks, blocks, blocks, P(),
    )
    return jax.shard_map(
        body,
        mesh=mesh,
        in_specs=placed,
        out_specs=(P("lev", "sub", None), blocks, blocks),
        check_vma=False,
    )
```

time: 175 us -> 130 us (0.74)
  local copies, waits for them, and re-layouts: 26.4 us -> 4.63 us
  waiting for transfers between devices: 12.1 us -> 0 us
  starting transfers between devices: 7.06 us -> 0 us
  other arithmetic: 4.12 us -> 0 us
  Pallas kernels: 123 us -> 125 us
    all_to_all x1 -> x0, waiting for transfers between devices: 12.1 us -> none  [body(): lax.all_to_all(pieces.reshape(NDEV, -1), ('lev', 'sub'), split_axis=0, co...]
    reshape x3 -> x1, local copies, waits for them, and re-layouts: 11.1 us -> 1.9 us  [body(): control.reshape(LEV // NLEV, NY // NSUB, NXB * NDEV)]
    all_to_all x1 -> x0, starting transfers between devices: 7.06 us -> none  [body(): lax.all_to_all(pieces.reshape(NDEV, -1), ('lev', 'sub'), split_axis=0, co...]
    transpose x1 -> x0, local copies, waits for them, and re-layouts: 6.14 us -> none  [body(): control.reshape(NXB, NLEV, LEV // NLEV, NSUB, NY // NSUB)]
    unnamed x11 -> x9, local copies, waits for them, and re-layouts: 4.78 us -> 2.72 us
    all_to_all x3 -> x0, local copies, waits for them, and re-layouts: 2.06 us -> none  [body(): lax.all_to_all(pieces.reshape(NDEV, -1), ('lev', 'sub'), split_axis=0, co...]
  transfers between devices with their start and end apart: 1 -> 0, of which waited for: 1 -> 0; matrix products, arithmetic and copies ran while one was open for 0% -> 0% of each run, Pallas kernels for 0% -> 0%
where the time goes in v2:
time: 130 us
  Pallas kernels  125 us (96%)
  local copies, waits for them, and re-layouts  4.63 us (4%)
    pallas_call x1, Pallas kernels, body(): pl.pallas_call(kernel, out_shape=(jax.ShapeDtypeStruct((4, 8, NXB * NDEV)...  125 us
    unnamed x9, local copies, waits for them, and re-layouts  2.72 us

profile of v2, /device:TPU:1, one launch (start us, length us, event | category | flops | bytes accessed | tf_op | source)
XLA Modules:
  0.0 130.2 jit_solution(16232210801404737806)
XLA Ops:
  0.6 0.0 copy-start.2
  0.6 0.7 copy-done.2
  1.3 0.7 copy.12.lx_ref
  2.0 124.9 %shard_map.112 = (f32[4,8,3072]{2,1,0:T(8,128)}, f32[768,128]{1,0:T(8,128)}, f32[1,8192]{1,0:T(1,128)}) custom-call(f32[8,4]{1,0:T(8,128)} %copy.12.lx_ref, f32[24,32]{1,0:T(8,128)} %ly_ref.1, f32[24,128]{1,0:T(8,128)} %lz_ref.1, f32[768,128]{1,0:T(8,128)} %bitcast.6, bf16[32,8192]{1,0:T(8,128)(2,1)} %prof_ref.1, f32[64,128]{1,0:T(8,128)} %bitcast.8, ...), custom_call_target="tpu_custom_call" | custom-call | tf_op jit(solution)/shard_map/pallas_call | solution.py:514
  126.9 0.0 copy-start
  126.9 1.9 %reshape.31 = f32[8,4,3072]{2,1,0:T(4,128)} reshape(f32[4,8,3072]{2,1,0:T(8,128)} %get-tuple-element.6) | data formatting | bytes 786432 | tf_op jit(solution)/shard_map/reshape | solution.py:572
  128.8 0.0 copy-done
  128.8 0.0 copy-start.1
  128.8 0.7 copy.15
  129.5 0.0 copy-done.1
  129.5 0.6 copy.16
Async XLA Ops:
  0.6 0.7 copy-start.2
  126.9 1.9 %copy-start = (f32[768,128]{1,0:T(8,128)S(1)}, f32[768,128]{1,0:T(8,128)}, u32[]{:S(2)}) copy-start(f32[768,128]{1,0:T(8,128)} %get-tuple-element.7) | copy-start | bytes 1179652
  128.8 0.8 copy-start.1

commit v3 on v2

--- a/solution.py
+++ b/solution.py
@@ -31,13 +31,13 @@
     return below * jnp.sqrt(below) / jnp.sqrt(jnp.sqrt(1.0 + square))
 
 
-def chunked_loop(count, unroll, body):
+def chunked_loop(start, end, unroll, body):
     def step(i, carry):
         for k in range(unroll):
             body(i * unroll + k)
         return carry
 
-    lax.fori_loop(0, count // unroll, step, 0)
+    lax.fori_loop(start // unroll, end // unroll, step, 0)
 
 
 def split(value):
@@ -106,49 +106,51 @@
         lax.broadcasted_iota(jnp.int32, (4, 128), 0)
         == lax.rem(lax.broadcasted_iota(jnp.int32, (4, 128), 1), 4)
     ).astype(F32)
-    own = jnp.dot(
-        lx_ref[...], pick4, precision=lax.Precision.HIGHEST, preferred_element_type=F32
+    own = lax.dot_general(
+        lx_ref[...], pick4, (((0,), (0,)), ((), ())),
+        precision=lax.Precision.HIGHEST, preferred_element_type=F32,
     )
     own_at = lax.broadcasted_iota(jnp.int32, (8, 128), 1) // 4
     own = jnp.where(own_at == lax.broadcasted_iota(jnp.int32, (8, 128), 0), own, 0.0)
     ms[:, 1, :] = jnp.broadcast_to(jnp.sum(own, axis=0, keepdims=True), (NDEV, 128))
 
-    def pack(i, carry):
+    def pack(i):
         at = pl.ds(pl.multiple_of(i * 128, 128), 128)
         w = prof_ref[:, at].astype(F32) * live_ref[pl.ds(i, 1), :]
         top, bottom = w[:16], w[16:]
         ws[2 * i] = jnp.where(low_half, top, pltpu.roll(bottom, CAP, 1)).astype(BF16)
         ws[2 * i + 1] = jnp.where(low_half, pltpu.roll(top, CAP, 1), bottom).astype(BF16)
-        return carry
-
-    lax.fori_loop(0, TILES, pack, 0)
+
+    chunked_loop(0, TILES, 4, pack)
     pl.semaphore_wait(barrier, NDEV - 1)
 
     pair, core = me // 2, lax.rem(me, 2)
     PAIRS = TILES // GROUPS
 
+    def send_meta(k, carry):
+        to = other(k)
+        pltpu.make_async_remote_copy(
+            src_ref=ms.at[to], dst_ref=ml.at[me], send_sem=meta_send.at[0],
+            recv_sem=meta_recv.at[0], device_id=device(to), device_id_type=MESH,
+        ).start()
+        return carry
+
     def send_block(kp, to_core):
-        to_pair = lax.rem(pair + kp, TILES)
-        to = 2 * to_pair + to_core
+        to = 2 * lax.rem(pair + kp, TILES) + to_core
         group = kp // PAIRS
-        pltpu.make_async_remote_copy(
-            src_ref=ms.at[to], dst_ref=ml.at[me],
-            send_sem=meta_send.at[group], recv_sem=meta_recv.at[group],
-            device_id=device(to), device_id_type=MESH,
-        ).start()
         pltpu.make_async_remote_copy(
             src_ref=ws.at[to], dst_ref=wl.at[me],
             send_sem=obs_send.at[group], recv_sem=obs_recv.at[group],
             device_id=device(to), device_id_type=MESH,
         ).start()
 
-    send_block(0, 1 - core)
-
     def send_pair(kp, carry):
         send_block(kp, core)
         send_block(kp, 1 - core)
         return carry
 
+    lax.fori_loop(1, NDEV, send_meta, 0)
+    send_block(0, 1 - core)
     lax.fori_loop(1, TILES, send_pair, 0)
     ml[me] = ms[me]
     wl[me] = ws[me]
@@ -166,9 +168,27 @@
     decay_z = jnp.exp(-1.0 / lz_ref[...])
     gain_z = gain_of(decay_z)
 
+    wait_all(ms.at[rest], ml.at[rest], meta_send.at[0], meta_recv.at[0])
+
+    lengths = ml[:, 1, :]
+    k_id = lax.broadcasted_iota(jnp.int32, (128, 128), 0)
+    y_id = lax.broadcasted_iota(jnp.int32, (128, 128), 1)
+    mine = (lax.rem(k_id, NSUB) == y_id // 4).astype(F32)
+    for row in range(8):
+        pick = (k_id == row * 4 + lax.rem(y_id, 4)).astype(F32)
+        spread_row = jnp.dot(
+            lengths, pick, precision=lax.Precision.HIGHEST, preferred_element_type=F32
+        )
+        rows = jnp.sum((spread_row * mine).reshape(NLEV, NSUB, 128), axis=1)
+        lenx_ref[pl.ds(row, NLEV, stride=8), :] = rows
+    decay_x = jnp.exp(-1.0 / lenx_ref[...])
+    gain_x = gain_of(decay_x)
+    dec_ref[...] = decay_x
+    gain_ref[...] = gain_x
+
     place = lax.broadcasted_iota(jnp.int32, (256, 128), 0).astype(F32).astype(BF16)
 
-    def widen(kp, carry):
+    def widen(kp):
         i = lax.rem(pair - kp + TILES, TILES)
         at = pl.ds(pl.multiple_of(i * 128, 128), 128)
         even, odd = wl[2 * i].astype(F32), wl[2 * i + 1].astype(F32)
@@ -184,53 +204,36 @@
             wide[pl.ds(c * LEV, LEV), at] = jnp.where(column == c, w, jnp.zeros_like(w))
         spot = jnp.broadcast_to(spot, (256, 128)).astype(BF16)
         rowhot[:, at] = jnp.where(place == spot, jnp.ones_like(place), jnp.zeros_like(place))
-        return carry
 
     for group in range(GROUPS):
         blocks = pl.ds(0, 2 * PAIRS - (group == 0))
-        wait_all(ms.at[blocks], ml.at[blocks], meta_send.at[group], meta_recv.at[group])
         wait_all(ws.at[blocks], wl.at[blocks], obs_send.at[group], obs_recv.at[group])
-        lax.fori_loop(group * PAIRS, (group + 1) * PAIRS, widen, 0)
-
-    lengths = ml[:, 1, :]
-    k_id = lax.broadcasted_iota(jnp.int32, (128, 128), 0)
-    y_id = lax.broadcasted_iota(jnp.int32, (128, 128), 1)
-    mine = (lax.rem(k_id, NSUB) == y_id // 4).astype(F32)
-    for row in range(8):
-        pick = (k_id == row * 4 + lax.rem(y_id, 4)).astype(F32)
-        spread_row = jnp.dot(
-            lengths, pick, precision=lax.Precision.HIGHEST, preferred_element_type=F32
-        )
-        rows = jnp.sum((spread_row * mine).reshape(NLEV, NSUB, 128), axis=1)
-        lenx_ref[pl.ds(row, NLEV, stride=8), :] = rows
-    decay_x = jnp.exp(-1.0 / lenx_ref[...])
-    gain_x = gain_of(decay_x)
-    dec_ref[...] = decay_x
-    gain_ref[...] = gain_x
-
-    level = pl.ds(sub_i, 1)
-    a = dec_ref[level, :]
-    g = gain_ref[level, :]
-    up = [a]
-    for _ in range(NXB - 1):
-        up.append(up[-1] * a)
-
-    def sweep(values):
-        total = jnp.zeros_like(a)
-        out = []
-        for value in values:
-            total = a * total + g * value
-            out.append(total)
-        return out
-
-    block_decay = up[-1]
-    p1 = sweep(up[::-1])[::-1]
-    q1 = sweep(p1)
-    q2 = sweep(up[::-1])
-    r1 = sweep(q1[::-1])
-    r2 = sweep(q2[::-1])
-    for index, value in enumerate((block_decay, p1[0], q1[-1], q2[-1], r1[-1], r2[-1])):
-        resp_ref[pl.ds(index, 1), :] = value
+        chunked_loop(group * PAIRS, (group + 1) * PAIRS, 4, widen)
+
+    def answer():
+        level = pl.ds(sub_i, 1)
+        a = dec_ref[level, :]
+        g = gain_ref[level, :]
+        up = [a]
+        for _ in range(NXB - 1):
+            up.append(up[-1] * a)
+
+        def sweep(values):
+            total = jnp.zeros_like(a)
+            out = []
+            for value in values:
+                total = a * total + g * value
+                out.append(total)
+            return out
+
+        block_decay = up[-1]
+        p1 = sweep(up[::-1])[::-1]
+        q1 = sweep(p1)
+        q2 = sweep(up[::-1])
+        r1 = sweep(q1[::-1])
+        r2 = sweep(q2[::-1])
+        for index, value in enumerate((block_decay, p1[0], q1[-1], q2[-1], r1[-1], r2[-1])):
+            resp_ref[pl.ds(index, 1), :] = value
 
     CHUNK = 2048
 
@@ -328,7 +331,9 @@
 
     def exchange_one(turn, field):
         for z in range(LEV):
-            tx1[turn, z // 2, pl.ds(z % 2 * NXB, NXB), :] = field[pl.ds(z, NXB, stride=LEV), :]
+            group, inner = z // 8, z % 8
+            at = pl.ds(group % 2 * NXB, NXB)
+            tx1[turn, inner * 2 + group // 2, at, :] = field[pl.ds(z, NXB, stride=LEV), :]
 
         def go(k, carry):
             to = lax.rem(part + k, 16)
@@ -342,46 +347,47 @@
         lax.fori_loop(1, 16, go, 0)
         ta[turn, part] = tx1[turn, part]
 
-    sub4 = lax.broadcasted_iota(jnp.int32, (1, 8, 1), 1) < 4
-    to_lev = part // 4
-    own_rows = lev_i == to_lev
+    inner_lev, first_lev = part // 2, lax.rem(part, 2) * 2
+    own_rows = lev_i // 2 == lax.rem(part, 2)
     slot_two = pl.ds(pl.multiple_of(group_x * 384, 384), 384)
 
     def exchange_two(turn):
         fifteen = pl.ds(0, 15)
         wait_all(ta.at[turn, fifteen], ta.at[turn, fifteen], one_send.at[turn], one_recv.at[turn])
-        lower = ta[turn, :, pl.ds(0, NXB), :].reshape(16 * NXB, 128).T.reshape(16, 8, 384)
-        upper = ta[turn, :, pl.ds(NXB, NXB), :].reshape(16 * NXB, 128).T.reshape(16, 8, 384)
-        even = jnp.where(sub4, lower, pltpu.roll(upper, 4, 1))
-        odd = jnp.where(sub4, pltpu.roll(lower, 4, 1), upper)
-        tx2[turn] = jnp.stack([even, odd], axis=1).reshape(NSUB, 8, 384)
-
-        def send_rows(to):
+        for which in range(2):
+            block = ta[turn, :, pl.ds(which * NXB, NXB), :].reshape(16 * NXB, 128)
+            tx2[turn, pl.ds(which * NSUB, NSUB)] = block.T.reshape(NSUB, 4, 384)
+
+        def send_rows(which, to):
             pltpu.make_async_remote_copy(
-                src_ref=tx2.at[turn, to],
-                dst_ref=tb.at[turn, lax.rem(part, 4), :, slot_two],
+                src_ref=tx2.at[turn, which * NSUB + to], dst_ref=tb.at[turn, inner_lev, :, slot_two],
                 send_sem=two_send.at[turn], recv_sem=two_recv.at[turn],
-                device_id=(to_lev, to), device_id_type=MESH,
+                device_id=(first_lev + which, to), device_id_type=MESH,
             ).start()
 
         def go(k, carry):
-            send_rows(lax.rem(sub_i + k, NSUB))
+            to = lax.rem(sub_i + k, NSUB)
+            send_rows(0, to)
+            send_rows(1, to)
             return carry
 
         lax.fori_loop(1, NSUB, go, 0)
 
         @pl.when(jnp.logical_not(own_rows))
         def _():
-            send_rows(sub_i)
+            send_rows(0, sub_i)
+            send_rows(1, sub_i)
 
         @pl.when(own_rows)
         def _():
-            tb[turn, lax.rem(part, 4), :, slot_two] = tx2[turn, sub_i]
+            mine = lax.rem(lev_i, 2)
+            send_rows(1 - mine, sub_i)
+            tb[turn, inner_lev, :, slot_two] = tx2[turn, mine * NSUB + sub_i]
 
     def finish_two(turn):
         @pl.when(own_rows)
         def _():
-            most = tx2.at[turn, pl.ds(0, NSUB - 1)]
+            most = tx2.at[turn, pl.ds(0, 2 * NSUB - 1)]
             wait_all(most, most, two_send.at[turn], two_recv.at[turn])
 
         @pl.when(jnp.logical_not(own_rows))
@@ -410,8 +416,8 @@
 
         lax.fori_loop(1, NDEV, send_edges, 0)
         el[turn, me] = es[turn, sub_i]
-        if turn == 1:
-            exchange_two(0)
+        if turn == 0:
+            answer()
         wait_all(el.at[turn, rest], el.at[turn, rest], edge_send.at[turn], edge_recv.at[turn])
 
         e1, e2 = el[turn, :, 0, :], el[turn, :, 1, :]
@@ -484,6 +490,7 @@
     observe(y0, zrow0)
     z0 = zrow0[...]
     share(0, [dot(x0[...], x0[...]), dot(z0, z0)])
+    exchange_two(0)
     spread(zrow0, False)
     covariance(1, x1, y1)
     rr0, zz0 = collect(0, 2)
@@ -514,7 +521,7 @@
     control, increment, departures = pl.pallas_call(
         kernel,
         out_shape=(
-            jax.ShapeDtypeStruct((4, 8, NXB * NDEV), F32),
+            jax.ShapeDtypeStruct((8, 4, NXB * NDEV), F32),
             jax.ShapeDtypeStruct((CELLS, 128), F32),
             jax.ShapeDtypeStruct((1, NOBS), F32),
         ),
@@ -555,21 +562,22 @@
             pltpu.VMEM((2, NDEV, 1, 128), F32),
             pltpu.VMEM((2, 16, 2 * NXB, 128), F32),
             pltpu.VMEM((2, 16, 2 * NXB, 128), F32),
-            pltpu.VMEM((2, NSUB, 8, 384), F32),
-            pltpu.VMEM((2, 4, 8, NXB * NDEV), F32),
+            pltpu.VMEM((2, 2 * NSUB, 4, 384), F32),
+            pltpu.VMEM((2, 8, 4, NXB * NDEV), F32),
         ]
-        + [pltpu.SemaphoreType.DMA((GROUPS,))] * 4
+        + [pltpu.SemaphoreType.DMA((1,))] * 2
+        + [pltpu.SemaphoreType.DMA((GROUPS,))] * 2
         + [pltpu.SemaphoreType.DMA((2,))] * 10,
         compiler_params=pltpu.CompilerParams(
             collective_id=0, has_side_effects=True, vmem_limit_bytes=56 << 20
         ),
     )(
-        length_x, length_y, length_z, sigma.reshape(CELLS, 128), obs_profile,
+        length_x.T, length_y, length_z, sigma.reshape(CELLS, 128), obs_profile,
         obs_scale.reshape(TILES, 128), innovation.reshape(TILES, 128),
         obs_column.reshape(TILES, 128), obs_count,
     )
     return (
-        control.reshape(LEV // NLEV, NY // NSUB, NXB * NDEV),
+        control,
         increment.reshape(NXB, LEV, NY),
         departures.reshape(NOBS),
     )

time: 130 us -> 103 us (0.79)
  Pallas kernels: 125 us -> 99.3 us
  local copies, waits for them, and re-layouts: 4.63 us -> 3.2 us
    pallas_call x1, Pallas kernels: 125 us -> 99.3 us  [body(): pl.pallas_call(kernel, out_shape=(jax.ShapeDtypeStruct((8, 4, NXB * NDEV)...]
    reshape x1 -> x0, local copies, waits for them, and re-layouts: 1.9 us -> none  [body(): control.reshape(LEV // NLEV, NY // NSUB, NXB * NDEV)]
    unnamed x9 -> x7, local copies, waits for them, and re-layouts: 2.72 us -> 3.2 us
where the time goes in v3:
time: 103 us
  Pallas kernels  99.3 us (96%)
  local copies, waits for them, and re-layouts  3.2 us (3%)
    pallas_call x1, Pallas kernels, body(): pl.pallas_call(kernel, out_shape=(jax.ShapeDtypeStruct((8, 4, NXB * NDEV)...  99.3 us
    unnamed x7, local copies, waits for them, and re-layouts  3.2 us

profile of v3, /device:TPU:1, one launch (start us, length us, event | category | flops | bytes accessed | tf_op | source)
XLA Modules:
  0.0 103.2 jit_solution(5732894504090146352)
XLA Ops:
  0.6 99.3 %shard_map.112 = (f32[8,4,3072]{2,1,0:T(4,128)}, f32[768,128]{1,0:T(8,128)}, f32[1,8192]{1,0:T(1,128)}) custom-call(f32[4,8]{1,0:T(4,128)} %bitcast.13, f32[24,32]{1,0:T(8,128)} %ly_ref.1, f32[24,128]{1,0:T(8,128)} %lz_ref.1, f32[768,128]{1,0:T(8,128)} %bitcast.7, bf16[32,8192]{1,0:T(8,128)(2,1)} %prof_ref.1, f32[64,128]{1,0:T(8,128)} %bitcast.9, ...), custom_call_target="tpu_custom_call" | custom-call | tf_op jit(solution)/shard_map/pallas_call | solution.py:521
  100.0 0.0 copy-start
  100.0 1.8 %copy.15 = f32[8,4,3072]{2,1,0:T(4,128)} copy(f32[8,4,3072]{2,1,0:T(4,128)} %get-tuple-element.12) | data formatting | bytes 786432
  101.8 0.0 copy-done
  101.8 0.0 copy-start.1
  101.8 0.7 copy.16
  102.5 0.0 copy-done.1
  102.6 0.6 copy.17
Async XLA Ops:
  100.0 1.8 %copy-start = (f32[768,128]{1,0:T(8,128)S(1)}, f32[768,128]{1,0:T(8,128)}, u32[]{:S(2)}) copy-start(f32[768,128]{1,0:T(8,128)} %get-tuple-element.7) | copy-start | bytes 1179652
  101.8 0.8 copy-start.1

commit v4 on v3

--- a/solution.py
+++ b/solution.py
@@ -40,19 +40,14 @@
     lax.fori_loop(start // unroll, end // unroll, step, 0)
 
 
-def split(value):
-    high = value.astype(BF16)
-    return high, (value - high.astype(F32)).astype(BF16)
-
-
 def kernel(
-    lx_ref, ly_ref, lz_ref, sigma_ref, prof_ref, scale_ref, raw_ref, col_ref, count_ref,
+    lx_ref, ly_ref, lz_ref, sigma_hbm, prof_hbm, scale_ref, raw_ref, col_ref, count_ref,
     control_ref, increment_ref, dep_ref,
-    live_ref, ms, ws, wl, ml, wide, rowhot, innov_ref, lenx_ref, dec_ref, gain_ref, resp_ref,
-    pw, gy_ref, v, ubuf, vbuf, x0, y0, x1, y1, tacc, fth, ftl, zs,
-    es, el, cs, cr, cl, sc_src, sc_land, tx1, ta, tx2, tb,
+    sigma_ref, prof_ref, live_ref, ms, ws, wl, ml, wide, rowhot, innov_ref, lenx_ref, dec_ref, gain_ref, resp_ref,
+    pw, gy_ref, v, ubuf, vbuf, x0, y0, x1, y1, res, tacc, fth, zs,
+    es, el, cs, cr, cl, sc_src, sc_land, tx1_0, ta_0, tx1_1, ta_1, tx2, tb, rows,
     meta_send, meta_recv, obs_send, obs_recv, edge_send, edge_recv, back_send, back_recv,
-    sc_send, sc_recv, one_send, one_recv, two_send, two_recv,
+    sc_send, sc_recv, one_send, one_recv, two_send, two_recv, load_sem,
 ):
     lev_i = lax.axis_index("lev")
     sub_i = lax.axis_index("sub")
@@ -64,6 +59,10 @@
     def other(k):
         return lax.rem(me + k, NDEV)
 
+    load_prof = pltpu.make_async_copy(prof_hbm, prof_ref, load_sem.at[0])
+    load_sigma = pltpu.make_async_copy(sigma_hbm, sigma_ref, load_sem.at[1])
+    load_prof.start()
+    load_sigma.start()
     barrier = pltpu.get_barrier_semaphore()
 
     def greet(k, carry):
@@ -121,6 +120,7 @@
         ws[2 * i] = jnp.where(low_half, top, pltpu.roll(bottom, CAP, 1)).astype(BF16)
         ws[2 * i + 1] = jnp.where(low_half, pltpu.roll(top, CAP, 1), bottom).astype(BF16)
 
+    load_prof.wait()
     chunked_loop(0, TILES, 4, pack)
     pl.semaphore_wait(barrier, NDEV - 1)
 
@@ -155,15 +155,16 @@
     ml[me] = ms[me]
     wl[me] = ws[me]
 
+    load_sigma.wait()
     decay_y = jnp.exp(-1.0 / ly_ref[...])
     gain_y = gain_of(decay_y).T
     decay_y = decay_y.T
     for c in range(NXB):
-        rows = pl.ds(c * LEV, LEV)
-        gy_ref[rows, :] = jnp.broadcast_to(gain_y[:, c:c + 1], (LEV, 128))
+        cells = pl.ds(c * LEV, LEV)
+        gy_ref[cells, :] = jnp.broadcast_to(gain_y[:, c:c + 1], (LEV, 128))
         power = jnp.broadcast_to(decay_y[:, c:c + 1], (LEV, 128))
         for k in range(7):
-            pw[k, rows, :] = power
+            pw[k, cells, :] = power
             power = power * power
     decay_z = jnp.exp(-1.0 / lz_ref[...])
     gain_z = gain_of(decay_z)
@@ -179,8 +180,8 @@
         spread_row = jnp.dot(
             lengths, pick, precision=lax.Precision.HIGHEST, preferred_element_type=F32
         )
-        rows = jnp.sum((spread_row * mine).reshape(NLEV, NSUB, 128), axis=1)
-        lenx_ref[pl.ds(row, NLEV, stride=8), :] = rows
+        of_levels = jnp.sum((spread_row * mine).reshape(NLEV, NSUB, 128), axis=1)
+        lenx_ref[pl.ds(row, NLEV, stride=8), :] = of_levels
     decay_x = jnp.exp(-1.0 / lenx_ref[...])
     gain_x = gain_of(decay_x)
     dec_ref[...] = decay_x
@@ -235,37 +236,22 @@
         for index, value in enumerate((block_decay, p1[0], q1[-1], q2[-1], r1[-1], r2[-1])):
             resp_ref[pl.ds(index, 1), :] = value
 
-    CHUNK = 2048
-
-    def spread(source, exact):
-        tacc[...] = jnp.zeros_like(tacc)
-
-        def step(i, carry):
-            at = pl.ds(pl.multiple_of(i * CHUNK, CHUNK), CHUNK)
-            hot = rowhot[:, at]
-            parts = split(source[:, at])
-            if exact:
-                parts = parts[:1]
-            total = tacc[...]
-            for part in parts:
-                total += lax.dot_general(
-                    wide[:, at], hot * part, (((1,), (1,)), ((), ())),
-                    preferred_element_type=F32,
-                )
-            tacc[...] = total
-            return carry
-
-        lax.fori_loop(0, NOBS // CHUNK, step, 0)
+    CHUNK = 4096
+
+    def spread(source):
+        tacc[...] = lax.dot_general(
+            wide[...], rowhot[...] * source[...].astype(BF16), (((1,), (1,)), ((), ())),
+            preferred_element_type=F32,
+        )
 
     def observe(field, out):
         side = jnp.concatenate([field[pl.ds(0, WROWS), :], field[pl.ds(WROWS, WROWS), :]], axis=1)
-        fth[...], ftl[...] = split(side.T)
+        fth[...] = side.astype(BF16).T
 
         def step(i, carry):
             at = pl.ds(pl.multiple_of(i * CHUNK, CHUNK), CHUNK)
             w = wide[:, at]
             got = jnp.dot(fth[...], w, preferred_element_type=F32)
-            got += jnp.dot(ftl[...], w, preferred_element_type=F32)
             out[:, at] = jnp.sum(got * rowhot[:, at].astype(F32), axis=0, keepdims=True)
             return carry
 
@@ -329,33 +315,40 @@
     part = lax.rem(sub_i, 16)
     group_x = lev_i * 2 + sub_i // 16
 
+    tx1, ta = (tx1_0, tx1_1), (ta_0, ta_1)
+
     def exchange_one(turn, field):
-        for z in range(LEV):
-            group, inner = z // 8, z % 8
-            at = pl.ds(group % 2 * NXB, NXB)
-            tx1[turn, inner * 2 + group // 2, at, :] = field[pl.ds(z, NXB, stride=LEV), :]
+        src, dst = tx1[turn], ta[turn]
+        for which in range(2):
+            for z in range(16):
+                core_of, inner = z // 8, z % 8
+                level = (core_of * 2 + which) * 8 + inner
+                rows[which, inner * 2 + core_of] = field[pl.ds(level, NXB, stride=LEV), :]
+        both = jnp.concatenate([rows[0], rows[1]], axis=1)
+        src[...] = both.astype(src.dtype)
 
         def go(k, carry):
             to = lax.rem(part + k, 16)
             pltpu.make_async_remote_copy(
-                src_ref=tx1.at[turn, to], dst_ref=ta.at[turn, part],
+                src_ref=src.at[to], dst_ref=dst.at[part],
                 send_sem=one_send.at[turn], recv_sem=one_recv.at[turn],
                 device_id=(lev_i, sub_i - part + to), device_id_type=MESH,
             ).start()
             return carry
 
         lax.fori_loop(1, 16, go, 0)
-        ta[turn, part] = tx1[turn, part]
+        dst[part] = src[part]
 
     inner_lev, first_lev = part // 2, lax.rem(part, 2) * 2
     own_rows = lev_i // 2 == lax.rem(part, 2)
     slot_two = pl.ds(pl.multiple_of(group_x * 384, 384), 384)
 
     def exchange_two(turn):
-        fifteen = pl.ds(0, 15)
-        wait_all(ta.at[turn, fifteen], ta.at[turn, fifteen], one_send.at[turn], one_recv.at[turn])
+        most = ta[turn].at[pl.ds(0, 15)]
+        wait_all(most, most, one_send.at[turn], one_recv.at[turn])
+        landed = ta[turn][...].astype(F32)
         for which in range(2):
-            block = ta[turn, :, pl.ds(which * NXB, NXB), :].reshape(16 * NXB, 128)
+            block = landed[:, which * NXB:(which + 1) * NXB, :].reshape(16 * NXB, 128)
             tx2[turn, pl.ds(which * NSUB, NSUB)] = block.T.reshape(NSUB, 4, 384)
 
         def send_rows(which, to):
@@ -394,7 +387,7 @@
         def _():
             wait_all(tx2.at[turn], tx2.at[turn], two_send.at[turn], two_recv.at[turn])
 
-    def covariance(turn, x_out, y_out):
+    def covariance(turn, x_out, y_out, after):
         v[pl.ds(0, WROWS), :] = tacc[:, pl.ds(0, 128)] * sigma_ref[pl.ds(0, WROWS), :]
         v[pl.ds(WROWS, WROWS), :] = tacc[:, pl.ds(128, 128)] * sigma_ref[pl.ds(WROWS, WROWS), :]
         filter_z(v, ubuf, vbuf)
@@ -447,7 +440,7 @@
         wait_all(cl.at[turn, back], cl.at[turn, back], back_send.at[turn], back_recv.at[turn])
         sweep_x(v, ubuf, cl[turn, :, 0, :], False)
         sweep_x(ubuf, x_out, cl[turn, :, 1, :], True)
-        exchange_one(turn, x_out)
+        after(turn, x_out)
         sweep_x(x_out, vbuf, cl[turn, :, 2, :], False)
         sweep_x(vbuf, ubuf, cl[turn, :, 3, :], True)
         filter_y(ubuf, vbuf)
@@ -485,21 +478,29 @@
         return jnp.sum(jnp.sum(left * right, axis=0, keepdims=True), axis=1, keepdims=True)
 
     zrow0, zrow1 = zs.at[pl.ds(0, 1)], zs.at[pl.ds(1, 1)]
-    spread(innov_ref, True)
-    covariance(0, x0, y0)
+    spread(innov_ref)
+    covariance(0, x0, y0, exchange_one)
     observe(y0, zrow0)
     z0 = zrow0[...]
     share(0, [dot(x0[...], x0[...]), dot(z0, z0)])
     exchange_two(0)
-    spread(zrow0, False)
-    covariance(1, x1, y1)
-    rr0, zz0 = collect(0, 2)
-    alpha0 = rr0 / (rr0 + zz0)
-    x1[...] = (1.0 - alpha0) * x0[...] - alpha0 * x1[...]
+    spread(zrow0)
+    scalars = []
+
+    def residual(turn, field):
+        scalars.extend(collect(0, 2))
+        rr0, zz0 = scalars
+        alpha0 = rr0 / (rr0 + zz0)
+        scalars.append(alpha0)
+        res[...] = (1.0 - alpha0) * x0[...] - alpha0 * field[...]
+        exchange_one(turn, res)
+
+    covariance(1, x1, y1, residual)
+    rr0, zz0, alpha0 = scalars
     y1[...] = (1.0 - alpha0) * y0[...] - alpha0 * y1[...]
     observe(y1, zrow1)
     z1 = zrow1[...]
-    share(1, [dot(x1[...], x1[...]), dot(x1[...], x0[...]), dot(z1, z1), dot(z1, z0)])
+    share(1, [dot(res[...], res[...]), dot(res[...], x0[...]), dot(z1, z1), dot(z1, z0)])
     exchange_two(1)
     rr1, cross, zz1, zcross = collect(1, 4)
     beta = rr1 / rr0
@@ -510,7 +511,13 @@
     dep_ref[...] = old * z0 + alpha1 * z1 - innov_ref[...]
     finish_two(0)
     finish_two(1)
-    control_ref[...] = (old + alpha1 * (1.0 - alpha0)) * tb[0] - (alpha1 * alpha0) * tb[1]
+    control_ref[...] = old * tb[0] + alpha1 * tb[1]
+
+
+def hand_over(a_in, b_in, c_in, a_out, b_out, c_out):
+    a_out[...] = a_in[...]
+    b_out[...] = b_in[...]
+    c_out[...] = c_in[...]
 
 
 def body(
@@ -525,9 +532,11 @@
             jax.ShapeDtypeStruct((CELLS, 128), F32),
             jax.ShapeDtypeStruct((1, NOBS), F32),
         ),
-        in_specs=[vmem] * 9,
+        in_specs=[vmem] * 3 + [pl.BlockSpec(memory_space=pl.ANY)] * 2 + [vmem] * 4,
         out_specs=(vmem,) * 3,
         scratch_shapes=[
+            field,
+            pltpu.VMEM((LEV, NOBS), BF16),
             pltpu.VMEM((TILES, 128), F32),
             pltpu.VMEM((NDEV, 2, 128), F32),
             pltpu.VMEM((NDEV, 16, 128), BF16),
@@ -549,8 +558,8 @@
             field,
             field,
             field,
+            field,
             pltpu.VMEM((WROWS, 256), F32),
-            pltpu.VMEM((256, WROWS), BF16),
             pltpu.VMEM((256, WROWS), BF16),
             pltpu.VMEM((2, NOBS), F32),
             pltpu.VMEM((2, LEV, 4, 128), F32),
@@ -560,14 +569,17 @@
             pltpu.VMEM((2, LEV, 4, 128), F32),
             pltpu.VMEM((2, 1, 128), F32),
             pltpu.VMEM((2, NDEV, 1, 128), F32),
-            pltpu.VMEM((2, 16, 2 * NXB, 128), F32),
-            pltpu.VMEM((2, 16, 2 * NXB, 128), F32),
+            pltpu.VMEM((16, 2 * NXB, 128), F32),
+            pltpu.VMEM((16, 2 * NXB, 128), F32),
+            pltpu.VMEM((16, 2 * NXB, 128), BF16),
+            pltpu.VMEM((16, 2 * NXB, 128), BF16),
             pltpu.VMEM((2, 2 * NSUB, 4, 384), F32),
             pltpu.VMEM((2, 8, 4, NXB * NDEV), F32),
+            pltpu.VMEM((2, 16, NXB, 128), F32),
         ]
         + [pltpu.SemaphoreType.DMA((1,))] * 2
         + [pltpu.SemaphoreType.DMA((GROUPS,))] * 2
-        + [pltpu.SemaphoreType.DMA((2,))] * 10,
+        + [pltpu.SemaphoreType.DMA((2,))] * 11,
         compiler_params=pltpu.CompilerParams(
             collective_id=0, has_side_effects=True, vmem_limit_bytes=56 << 20
         ),
@@ -576,6 +588,17 @@
         obs_scale.reshape(TILES, 128), innovation.reshape(TILES, 128),
         obs_column.reshape(TILES, 128), obs_count,
     )
+    whole = pl.BlockSpec(memory_space=pltpu.VMEM)
+    control, increment, departures = pl.pallas_call(
+        hand_over,
+        out_shape=(
+            jax.ShapeDtypeStruct((8, 4, NXB * NDEV), F32),
+            jax.ShapeDtypeStruct((CELLS, 128), F32),
+            jax.ShapeDtypeStruct((1, NOBS), F32),
+        ),
+        in_specs=[whole] * 3,
+        out_specs=(whole,) * 3,
+    )(control, increment, departures)
     return (
         control,
         increment.reshape(NXB, LEV, NY),

time: 103 us -> 93.7 us (0.910)
  Pallas kernels: 99.3 us -> 92.8 us
  local copies, waits for them, and re-layouts: 3.2 us -> 0 us
    pallas_call x1, Pallas kernels: 99.3 us -> 90.8 us  [body(): pl.pallas_call(kernel, out_shape=(jax.ShapeDtypeStruct((8, 4, NXB * NDEV)...]
    unnamed x7 -> x0, local copies, waits for them, and re-layouts: 3.2 us -> none
    pallas_call x0 -> x1, Pallas kernels: none -> 2.02 us  [body(): pl.pallas_call(hand_over, out_shape=(jax.ShapeDtypeStruct((8, 4, NXB * ND...]
where the time goes in v4:
time: 93.7 us; the launch traced here: 93.5 us
  Pallas kernels  92.8 us (99%)
    pallas_call x1, Pallas kernels, body(): pl.pallas_call(kernel, out_shape=(jax.ShapeDtypeStruct((8, 4, NXB * NDEV)...  90.8 us
    pallas_call x1, Pallas kernels, body(): pl.pallas_call(hand_over, out_shape=(jax.ShapeDtypeStruct((8, 4, NXB * ND...  2.02 us

profile of v4, /device:TPU:1, one launch (start us, length us, event | category | flops | bytes accessed | tf_op | source)
XLA Modules:
  0.0 93.5 jit_solution(17725198281165199486)
XLA Ops:
  0.6 90.8 %shard_map.112 = (f32[8,4,3072]{2,1,0:T(4,128)}, f32[768,128]{1,0:T(8,128)}, f32[1,8192]{1,0:T(1,128)}) custom-call(f32[4,8]{1,0:T(4,128)} %bitcast.11, f32[24,32]{1,0:T(8,128)} %ly_ref.1, f32[24,128]{1,0:T(8,128)} %lz_ref.1, f32[768,128]{1,0:T(8,128)} %bitcast.7, bf16[32,8192]{1,0:T(8,128)(2,1)} %prof_hbm.1, f32[64,128]{1,0:T(8,128)} %bitcast.8, ...), custom_call_target="tpu_custom_call" | custom-call | tf_op jit(solution)/shard_map/pallas_call | solution.py:528
  91.5 2.0 %shard_map.113 = (f32[8,4,3072]{2,1,0:T(4,128)}, f32[768,128]{1,0:T(8,128)}, f32[1,8192]{1,0:T(1,128)}) custom-call(f32[8,4,3072]{2,1,0:T(4,128)} %get-tuple-element.9.a_in, f32[768,128]{1,0:T(8,128)} %get-tuple-element.10.b_in, f32[1,8192]{1,0:T(1,128)} %get-tuple-element.11.c_in), custom_call_target="tpu_custom_call" | custom-call | tf_op jit(solution)/shard_map/pallas_call | solution.py:592

commit v5 on v4

--- a/solution.py
+++ b/solution.py
@@ -323,9 +323,14 @@
             for z in range(16):
                 core_of, inner = z // 8, z % 8
                 level = (core_of * 2 + which) * 8 + inner
-                rows[which, inner * 2 + core_of] = field[pl.ds(level, NXB, stride=LEV), :]
-        both = jnp.concatenate([rows[0], rows[1]], axis=1)
-        src[...] = both.astype(src.dtype)
+                line = field[pl.ds(level, NXB, stride=LEV), :]
+                if turn == 0:
+                    src[inner * 2 + core_of, pl.ds(which * NXB, NXB), :] = line
+                else:
+                    rows[which, inner * 2 + core_of] = line
+        if turn == 1:
+            both = jnp.concatenate([rows[0], rows[1]], axis=1)
+            src[...] = both.astype(src.dtype)
 
         def go(k, carry):
             to = lax.rem(part + k, 16)

time: 93.7 us -> 93.6 us (level)
  no operation moved by 1% of the time
where the time goes in v5:
time: 93.6 us; the launch traced here: 93.5 us
  Pallas kernels  92.8 us (99%)
    pallas_call x1, Pallas kernels, body(): pl.pallas_call(kernel, out_shape=(jax.ShapeDtypeStruct((8, 4, NXB * NDEV)...  90.8 us
    pallas_call x1, Pallas kernels, body(): pl.pallas_call(hand_over, out_shape=(jax.ShapeDtypeStruct((8, 4, NXB * ND...  2.02 us

profile of v5, /device:TPU:1, one launch (start us, length us, event | category | flops | bytes accessed | tf_op | source)
XLA Modules:
  0.0 93.5 jit_solution(10260038416682198607)
XLA Ops:
  0.6 90.8 %shard_map.112 = (f32[8,4,3072]{2,1,0:T(4,128)}, f32[768,128]{1,0:T(8,128)}, f32[1,8192]{1,0:T(1,128)}) custom-call(f32[4,8]{1,0:T(4,128)} %bitcast.11, f32[24,32]{1,0:T(8,128)} %ly_ref.1, f32[24,128]{1,0:T(8,128)} %lz_ref.1, f32[768,128]{1,0:T(8,128)} %bitcast.7, bf16[32,8192]{1,0:T(8,128)(2,1)} %prof_hbm.1, f32[64,128]{1,0:T(8,128)} %bitcast.8, ...), custom_call_target="tpu_custom_call" | custom-call | tf_op jit(solution)/shard_map/pallas_call | solution.py:533
  91.4 2.0 %shard_map.113 = (f32[8,4,3072]{2,1,0:T(4,128)}, f32[768,128]{1,0:T(8,128)}, f32[1,8192]{1,0:T(1,128)}) custom-call(f32[8,4,3072]{2,1,0:T(4,128)} %get-tuple-element.9.a_in, f32[768,128]{1,0:T(8,128)} %get-tuple-element.10.b_in, f32[1,8192]{1,0:T(1,128)} %get-tuple-element.11.c_in), custom_call_target="tpu_custom_call" | custom-call | tf_op jit(solution)/shard_map/pallas_call | solution.py:597
